TPU v7x, 128 devices: a whole 4x4x4 slice. The times are simulated.
128 devices in a mesh: blk: 16 (over z, y), grid: 8 (over x, core).
Axes of the slice: x: 4, y: 4, z: 4, core: 2. Of those that a mesh axis runs over, the one named last changes fastest.
Arguments:
- queries: bfloat16 [81920, 32, 128], P(('blk', 'grid')), may hold values from -100 to 100
- keys: bfloat16 [81920, 8, 128], P(('blk', 'grid')), may hold values from -5 to 5
- values: bfloat16 [81920, 8, 128], P(('blk', 'grid')), may hold values from -40 to 40
- vert_blocks: int32 [8, 12], replicated, may hold values from 0 to 1279, as said below
- slash_offsets: int32 [8, 4], replicated, may hold values from 0 to 7, as said below
- far_blocks: int32 [8, 1280], replicated, may hold values from -1 to 1271, as said below
Outputs:
- attended: bfloat16 [81920, 32, 128], P(('blk', 'grid'))
Inputs may be any that keep to these rules, and one draw needn't show every extreme that they name: `vert_blocks`: each key head has 12 different vertical blocks. Over all heads together at most 1 vertical blocks lie among the 10 blocks of one device, and exactly 1 among those of some device. `slash_offsets`: each key head's list holds 4 different offsets, 0 among them; the list of some head holds 7. An entry far_blocks[h, b] is -1 or a block at most b - 8 that is not a vertical block of head h. The entries of all heads for the 10 query blocks of one device name at most 2 blocks among the 10 blocks of any one device, and exactly 2 for some pair of devices.
All inputs are finite; a program needn't handle non-finite values.
Results may differ from a plain program's by a relative error of at most 0.0046.
Values may be sent and summed in bfloat16 or wider, within the bound.
No kernel may reach another device: no remote copies, remote signals or barrier semaphores. Data moves between devices by JAX's collectives and lax.ppermute only.
A program may use at most 448 MiB of HBM per device.

v0:
```python
import jax
import jax.numpy as jnp
from jax import lax
from jax.sharding import PartitionSpec as P

BS = 64
NW = 8


def shifted(value, axis, steps):
    count = lax.axis_size(axis)
    first, last = (max(0, -steps), min(count, count - steps))
    return lax.ppermute(value, axis, [(source, source + steps) for source in range(first, last)])


def far_partial(q_tile, k_tile, v_tile, score_scale):
    scores = (
        jnp.einsum("...tgd,...kd->...tgk", q_tile, k_tile, preferred_element_type=jnp.float32)
        * score_scale
    )
    top_score = jnp.max(scores, axis=-1)
    weights = jnp.exp(scores - top_score[..., None])
    weight_sum = jnp.sum(weights, axis=-1)
    mixed_sum = jnp.einsum(
        "...tgk,...kd->...tgd",
        weights.astype(jnp.bfloat16),
        v_tile,
        preferred_element_type=jnp.float32,
    )
    partial_out = (mixed_sum / weight_sum[..., None]).astype(jnp.bfloat16)
    return (partial_out, top_score + jnp.log(weight_sum))


def earlier_count(labels):
    count_all = labels.shape[-1]
    same_label = labels[..., :, None] == labels[..., None, :]
    is_earlier = jnp.arange(count_all)[None, :] < jnp.arange(count_all)[:, None]
    return jnp.sum(same_label & is_earlier, axis=-1)


def route_tiles(tile_buf):
    return lax.all_to_all(tile_buf, ("blk", "grid"), split_axis=0, concat_axis=0, tiled=True)


def shards(queries, keys, values, vert_blocks, slash_offsets, far_blocks):
    tok_count, q_heads, head_dim = queries.shape
    kv_heads = keys.shape[1]
    group_size = q_heads // kv_heads
    block_len = BS
    window = NW
    block_count = tok_count // block_len
    vert_count = vert_blocks.shape[1]
    near_count = slash_offsets.shape[1]
    req_count = kv_heads * block_count
    device_count = lax.axis_size(("blk", "grid"))
    my_rank = lax.axis_index(("blk", "grid"))
    cap_far = max(2, 2 * req_count // device_count)
    cap_vert = max(1, (kv_heads * vert_count + device_count - 1) // device_count)
    score_scale = head_dim ** (-0.5)
    q_blocks = queries.reshape(block_count, block_len, kv_heads, group_size, head_dim)
    k_blocks = keys.reshape(block_count, block_len, kv_heads, head_dim)
    v_blocks = values.reshape(block_count, block_len, kv_heads, head_dim)
    rim_rows = (window - 1) * block_len
    rim_pair = jnp.stack([keys[tok_count - rim_rows :], values[tok_count - rim_rows :]])
    before = shifted(rim_pair, ("blk", "grid"), 1)
    ext_shape = (block_count + window - 1, block_len, kv_heads, head_dim)
    key_ext = jnp.concatenate([before[0], keys], axis=0).reshape(ext_shape)
    val_ext = jnp.concatenate([before[1], values], axis=0).reshape(ext_shape)
    vert_flat = vert_blocks.reshape(-1)
    vert_owner = vert_flat // block_count
    vert_rank = earlier_count(vert_owner)
    own_picks = (vert_owner[None, :] == my_rank) & (
        vert_rank[None, :] == jnp.arange(cap_vert)[:, None]
    )
    pick_index = jnp.sum(jnp.where(own_picks, jnp.arange(vert_flat.shape[0])[None, :], 0), axis=1)
    pick_valid = jnp.any(own_picks, axis=1)
    pick_head = pick_index // vert_count
    pick_local = jnp.clip(vert_flat[pick_index] - my_rank * block_count, 0, block_count - 1)
    own_keys = k_blocks[pick_local, :, pick_head]
    own_vals = v_blocks[pick_local, :, pick_head]
    own_pair = jnp.where(
        pick_valid[:, None, None, None], jnp.stack([own_keys, own_vals], axis=1), 0
    )
    all_pairs = lax.all_gather(own_pair, ("blk", "grid"), axis=0, tiled=True)
    vert_pos = vert_owner * cap_vert + vert_rank
    vert_kv = all_pairs[vert_pos].reshape(kv_heads, vert_count, 2, block_len, head_dim)
    my_far = lax.dynamic_slice_in_dim(far_blocks, my_rank * block_count, block_count, 1).reshape(-1)
    far_valid = my_far >= 0
    far_dest = jnp.where(far_valid, my_far // block_count, device_count)
    far_slot = earlier_count(far_dest)
    pick_dest = jnp.minimum(far_dest, device_count - 1)
    req_head = jnp.arange(req_count) // block_count
    req_block = jnp.arange(req_count) % block_count
    q_tiles = q_blocks[req_block, :, req_head]
    all_far = (
        far_blocks.reshape(kv_heads, device_count, block_count)
        .transpose(1, 0, 2)
        .reshape(device_count, req_count)
    )
    all_dest = jnp.where(all_far >= 0, all_far // block_count, device_count)
    all_slot = earlier_count(all_dest)
    serve_mask = (all_dest[:, None, :] == my_rank) & (
        all_slot[:, None, :] == jnp.arange(cap_far)[None, :, None]
    )
    serve_index = jnp.sum(jnp.where(serve_mask, jnp.arange(req_count)[None, None, :], 0), axis=2)
    serve_valid = jnp.any(serve_mask, axis=2)
    serve_block = jnp.take_along_axis(all_far, serve_index, axis=1)
    serve_local = jnp.clip(serve_block - my_rank * block_count, 0, block_count - 1)
    serve_head = serve_index // block_count
    serve_keys = k_blocks[serve_local, :, serve_head]
    serve_vals = v_blocks[serve_local, :, serve_head]
    send_pair = jnp.where(
        serve_valid[:, :, None, None, None], jnp.stack([serve_keys, serve_vals], axis=2), 0
    )
    got_pair = route_tiles(send_pair)
    chosen_pair = got_pair[pick_dest, far_slot]
    far_out, far_lse = far_partial(q_tiles, chosen_pair[:, 0], chosen_pair[:, 1], score_scale)
    far_out = far_out.reshape(kv_heads, block_count, block_len, group_size, head_dim)
    far_lse = far_lse.reshape(kv_heads, block_count, block_len, group_size)
    far_valid = far_valid.reshape(kv_heads, block_count)
    query_block = my_rank * block_count + jnp.arange(block_count)
    causal_ok = jnp.arange(block_len)[None, :] <= jnp.arange(block_len)[:, None]
    results = []
    for kv_head in range(kv_heads):
        offsets = slash_offsets[kv_head]
        near_index = jnp.arange(block_count)[:, None] + (window - 1) - offsets[None, :]
        near_keys = key_ext[:, :, kv_head][near_index]
        near_vals = val_ext[:, :, kv_head][near_index]
        q_here = q_blocks[:, :, kv_head]
        vert_keys = vert_kv[kv_head, :, 0]
        vert_vals = vert_kv[kv_head, :, 1]
        near_scores = (
            jnp.einsum("btgd,bikd->btgik", q_here, near_keys, preferred_element_type=jnp.float32)
            * score_scale
        )
        vert_scores = (
            jnp.einsum("btgd,ikd->btgik", q_here, vert_keys, preferred_element_type=jnp.float32)
            * score_scale
        )
        near_ok = query_block[:, None] - offsets[None, :] >= 0
        near_mask = near_ok[:, None, None, :, None] & (
            (offsets != 0)[None, None, None, :, None] | causal_ok[None, :, None, None, :]
        )
        vert_ok = (vert_blocks[kv_head][None, :] <= query_block[:, None] - window)[
            :, None, None, :, None
        ]
        scores = jnp.concatenate(
            [
                jnp.where(near_mask, near_scores, -jnp.inf),
                jnp.where(vert_ok, vert_scores, -jnp.inf),
            ],
            axis=3,
        )
        top_score = jnp.max(scores, axis=(3, 4))
        weights = jnp.exp(scores - top_score[..., None, None])
        weight_sum = jnp.sum(weights, axis=(3, 4))
        low_weights = weights.astype(jnp.bfloat16)
        mixed_sum = jnp.einsum(
            "btgik,bikd->btgd",
            low_weights[:, :, :, :near_count],
            near_vals,
            preferred_element_type=jnp.float32,
        )
        mixed_sum = mixed_sum + jnp.einsum(
            "btgik,ikd->btgd",
            low_weights[:, :, :, near_count:],
            vert_vals,
            preferred_element_type=jnp.float32,
        )
        local_out = mixed_sum / weight_sum[..., None]
        local_lse = top_score + jnp.log(weight_sum)
        far_ok = far_valid[kv_head][:, None, None]
        far_lse_here = far_lse[kv_head]
        joint_max = jnp.maximum(local_lse, jnp.where(far_ok, far_lse_here, local_lse))
        local_weight = jnp.exp(local_lse - joint_max)
        far_weight = jnp.where(far_ok, jnp.exp(far_lse_here - joint_max), 0.0)
        far_part = jnp.where(far_ok[..., None], far_out[kv_head].astype(jnp.float32), 0.0)
        merged = (local_weight[..., None] * local_out + far_weight[..., None] * far_part) / (
            local_weight + far_weight
        )[..., None]
        results.append(merged.astype(jnp.bfloat16))
    return jnp.stack(results, axis=2).reshape(tok_count, q_heads, head_dim)


def solution(mesh):
    placed = (
        P(("blk", "grid"), None, None),
        P(("blk", "grid"), None, None),
        P(("blk", "grid"), None, None),
        P(),
        P(),
        P(),
    )
    return jax.shard_map(
        shards,
        mesh=mesh,
        in_specs=placed,
        out_specs=P(("blk", "grid"), None, None),
        check_vma=False,
    )
```

profile of v0, /device:TPU:1, one launch (start us, length us, event | category | flops | bytes accessed | tf_op | source)
XLA Modules:
  0.0 439.5 jit_solution(8342461324813339549)
XLA Ops:
  38.4 7.3 %maximum_select_fusion = bf16[128,2,2,64,128]{4,3,2,1,0:T(8,128)(2,1)} fusion(bf16[128,2,1,64,128]{4,3,2,1,0:T(8,128)(2,1)} %bitcast.733, bf16[128,2,1,64,128]{4,3,2,1,0:T(8,128)(2,1)} %bitcast.732, pred[128,2]{1,0:T(8,128)(4,1)S(1)} %copy.287), kind=kLoop, calls=%fused_computation.67 | loop fusion | flops 8388608 | bytes 16777472 | tf_op jit(solution)/shard_map/jit(_where)/select_n | solution.py:112
  45.7 10.6 %all-to-all-start = ((bf16[128,2,2,64,128]{4,3,2,1,0:T(8,128)(2,1)}), bf16[128,2,2,64,128]{4,3,2,1,0:T(8,128)(2,1)}, u32[]{:S(2)}, u32[]{:S(2)}) async-start(bf16[128,2,2,64,128]{4,3,2,1,0:T(8,128)(2,1)} %maximum_select_fusion), calls=%async_computation | async-start | bytes 16777216 | tf_op jit(solution)/shard_map/all_to_all | solution.py:42
  58.6 6.9 %copy.282 = bf16[640,32,128]{2,0,1:T(8,128)(2,1)} copy(bf16[640,32,128]{2,1,0:T(8,128)(2,1)} %param.6) | data formatting | bytes 10485760 | tf_op args[0]
  66.0 9.7 %gather_fusion.2 = bf16[80,64,4,128]{3,1,2,0:T(8,128)(2,1)} fusion(bf16[10,64,8,4,128]{4,1,0,3,2:T(8,128)(2,1)} %bitcast.712, s32[80]{0:T(128)S(1)} %get-tuple-element.223), kind=kCustom, calls=%fused_computation.2 | custom fusion | bytes 10486400 | tf_op jit(solution)/shard_map/gather | solution.py:94
  98.2 6.8 %pad_maximum_fusion = bf16[1088,8,128]{2,1,0:T(8,128)(2,1)S(1)} fusion(bf16[640,8,128]{2,1,0:T(8,128)(2,1)S(1)} %copy-done.2, bf16[448,8,128]{2,1,0:T(8,128)(2,1)S(1)} %get-tuple-element.102), kind=kLoop, calls=%fused_computation.79 | loop fusion | flops 1114112 | bytes 4456448 | tf_op jit(solution)/shard_map/concatenate | solution.py:67
  183.6 9.1 %fusion.248 = (f32[10,64,4]{1,2,0:T(4,128)S(1)}, f32[10,64,4,12,64]{1,4,2,0,3:T(8,128)}) fusion(bf16[10,64,1,4,128]{4,1,0,3,2:T(8,128)(2,1)} %get-tuple-element.83, bf16[8,12,2,64,128]{4,3,2,1,0:T(8,128)(2,1)} %bitcast.741, pred[10,12]{0,1:T(8,128)(4,1)S(1)} %get-tuple-element.148), kind=kOutput, calls=%fused_computation.467 | convolution fusion | flops 509212160 | bytes 8726648 | tf_op jit(solution)/shard_map/btgd,ikd->btgik/dot_general | solution.py:137
  192.7 8.6 %fusion.21 = f32[10,64,4]{1,2,0:T(4,128)S(1)} fusion(f32[10,64,4,12,64]{1,4,2,0,3:T(8,128)} %get-tuple-element.184, f32[10,64,4]{1,2,0:T(4,128)S(1)} %reduce_max.183, f32[10,64,4,4,64]{1,4,2,3,0:T(8,128)S(1)} %bitcast.729), kind=kLoop, calls=%fused_computation.59 | loop fusion | flops 7861760 | bytes 10506240 | tf_op jit(solution)/shard_map/reduce_sum | solution.py:156
  205.9 9.2 %fusion.250 = (f32[10,64,4]{1,2,0:T(4,128)S(1)}, f32[10,64,4,12,64]{1,4,2,0,3:T(8,128)}) fusion(bf16[10,64,1,4,128]{4,1,0,3,2:T(8,128)(2,1)} %get-tuple-element.82, bf16[8,12,2,64,128]{4,3,2,1,0:T(8,128)(2,1)} %bitcast.742, pred[10,12]{0,1:T(8,128)(4,1)S(1)} %get-tuple-element.149), kind=kOutput, calls=%fused_computation.469 | convolution fusion | flops 509212160 | bytes 8726648 | tf_op jit(solution)/shard_map/btgd,ikd->btgik/dot_general | solution.py:137
  215.2 8.8 %fusion.19 = f32[10,64,4]{1,2,0:T(4,128)S(1)} fusion(f32[10,64,4,12,64]{1,4,2,0,3:T(8,128)} %get-tuple-element.188, f32[10,64,4]{1,2,0:T(4,128)S(1)} %reduce_max.186, f32[10,64,4,4,64]{1,4,2,3,0:T(8,128)S(1)} %bitcast.727), kind=kLoop, calls=%fused_computation.57 | loop fusion | flops 7861760 | bytes 10506240 | tf_op jit(solution)/shard_map/reduce_sum | solution.py:156
  228.6 9.2 %fusion.254 = (f32[10,64,4]{1,2,0:T(4,128)S(1)}, f32[10,64,4,12,64]{1,4,2,0,3:T(8,128)}) fusion(bf16[10,64,1,4,128]{4,1,0,3,2:T(8,128)(2,1)} %get-tuple-element.81, bf16[8,12,2,64,128]{4,3,2,1,0:T(8,128)(2,1)} %bitcast.743, pred[10,12]{0,1:T(8,128)(4,1)S(1)} %get-tuple-element.150), kind=kOutput, calls=%fused_computation.473 | convolution fusion | flops 509212160 | bytes 8726648 | tf_op jit(solution)/shard_map/btgd,ikd->btgik/dot_general | solution.py:137
  237.9 8.6 %fusion.17 = f32[10,64,4]{1,2,0:T(4,128)S(1)} fusion(f32[10,64,4,12,64]{1,4,2,0,3:T(8,128)} %get-tuple-element.196, f32[10,64,4]{1,2,0:T(4,128)S(1)} %reduce_max.189, f32[10,64,4,4,64]{1,4,2,3,0:T(8,128)S(1)} %bitcast.725), kind=kLoop, calls=%fused_computation.55 | loop fusion | flops 7861760 | bytes 10506240 | tf_op jit(solution)/shard_map/reduce_sum | solution.py:156
  250.4 9.1 %fusion.256 = (f32[10,64,4]{1,2,0:T(4,128)S(1)}, f32[10,64,4,12,64]{1,4,2,0,3:T(8,128)}) fusion(bf16[10,64,1,4,128]{4,1,0,3,2:T(8,128)(2,1)} %get-tuple-element.80, bf16[8,12,2,64,128]{4,3,2,1,0:T(8,128)(2,1)} %bitcast.744, pred[10,12]{0,1:T(8,128)(4,1)S(1)} %get-tuple-element.151), kind=kOutput, calls=%fused_computation.475 | convolution fusion | flops 509212160 | bytes 8726648 | tf_op jit(solution)/shard_map/btgd,ikd->btgik/dot_general | solution.py:137
  259.6 8.6 %fusion.15 = f32[10,64,4]{1,2,0:T(4,128)S(1)} fusion(f32[10,64,4,12,64]{1,4,2,0,3:T(8,128)} %get-tuple-element.200, f32[10,64,4]{1,2,0:T(4,128)S(1)} %reduce_max.192, f32[10,64,4,4,64]{1,4,2,3,0:T(8,128)S(1)} %bitcast.723), kind=kLoop, calls=%fused_computation.53 | loop fusion | flops 7861760 | bytes 10506240 | tf_op jit(solution)/shard_map/reduce_sum | solution.py:156
  271.6 7.6 %fusion.258 = (f32[10,64,4]{1,2,0:T(4,128)S(1)}, f32[10,64,4,12,64]{1,4,2,0,3:T(8,128)}) fusion(bf16[10,64,1,4,128]{4,1,0,3,2:T(8,128)(2,1)S(1)} %copy-done.23, bf16[8,12,2,64,128]{4,3,2,1,0:T(8,128)(2,1)} %bitcast.745, pred[10,12]{0,1:T(8,128)(4,1)S(1)} %get-tuple-element.152), kind=kOutput, calls=%fused_computation.477 | convolution fusion | flops 509212160 | bytes 8726648 | tf_op jit(solution)/shard_map/btgd,ikd->btgik/dot_general | solution.py:137
  279.3 8.9 %fusion.13 = f32[10,64,4]{1,2,0:T(4,128)S(1)} fusion(f32[10,64,4,12,64]{1,4,2,0,3:T(8,128)} %get-tuple-element.204, f32[10,64,4]{1,2,0:T(4,128)S(1)} %reduce_max.195, f32[10,64,4,4,64]{1,4,2,3,0:T(8,128)S(1)} %bitcast.721), kind=kLoop, calls=%fused_computation.51 | loop fusion | flops 7861760 | bytes 10506240 | tf_op jit(solution)/shard_map/reduce_sum | solution.py:156
  291.6 7.8 %fusion.252 = (f32[10,64,4]{1,2,0:T(4,128)S(1)}, f32[10,64,4,12,64]{1,4,2,0,3:T(8,128)}) fusion(bf16[10,64,1,4,128]{4,1,0,3,2:T(8,128)(2,1)S(1)} %copy-done.22, bf16[8,12,2,64,128]{4,3,2,1,0:T(8,128)(2,1)} %bitcast.746, pred[10,12]{0,1:T(8,128)(4,1)S(1)} %get-tuple-element.153), kind=kOutput, calls=%fused_computation.471 | convolution fusion | flops 509212160 | bytes 8726648 | tf_op jit(solution)/shard_map/btgd,ikd->btgik/dot_general | solution.py:137
  299.5 8.4 %fusion.11 = f32[10,64,4]{1,2,0:T(4,128)S(1)} fusion(f32[10,64,4,12,64]{1,4,2,0,3:T(8,128)} %get-tuple-element.192, f32[10,64,4]{1,2,0:T(4,128)S(1)} %reduce_max.198, f32[10,64,4,4,64]{1,4,2,3,0:T(8,128)S(1)} %bitcast.719), kind=kLoop, calls=%fused_computation.49 | loop fusion | flops 7861760 | bytes 10506240 | tf_op jit(solution)/shard_map/reduce_sum | solution.py:156
  307.9 7.7 %fusion.244 = (f32[10,64,4]{1,2,0:T(4,128)S(1)}, f32[10,64,4,12,64]{1,4,2,0,3:T(8,128)}) fusion(bf16[10,64,1,4,128]{4,1,0,3,2:T(8,128)(2,1)S(1)} %copy-done.20, bf16[8,12,2,64,128]{4,3,2,1,0:T(8,128)(2,1)} %bitcast.747, pred[10,12]{0,1:T(8,128)(4,1)S(1)} %get-tuple-element.147), kind=kOutput, calls=%fused_computation.463 | convolution fusion | flops 509212160 | bytes 8726648 | tf_op jit(solution)/shard_map/btgd,ikd->btgik/dot_general | solution.py:137
  315.7 8.3 %fusion.9 = f32[10,64,4]{1,2,0:T(4,128)S(1)} fusion(f32[10,64,4,12,64]{1,4,2,0,3:T(8,128)} %get-tuple-element.174, f32[10,64,4]{1,2,0:T(4,128)S(1)} %reduce_max.201, f32[10,64,4,4,64]{1,4,2,3,0:T(8,128)S(1)} %bitcast.715), kind=kLoop, calls=%fused_computation.47 | loop fusion | flops 7861760 | bytes 10506240 | tf_op jit(solution)/shard_map/reduce_sum | solution.py:156
  334.1 7.9 %fusion.125 = f32[10,64,4,128,1]{3,1,2,0,4:T(8,128)} fusion(bf16[8,12,2,64,128]{4,3,2,1,0:T(8,128)(2,1)} %bitcast.749, f32[10,64,4,12,64]{1,4,2,0,3:T(8,128)} %get-tuple-element.184, f32[10,64,4]{1,2,0:T(4,128)S(1)} %reduce_max.183, f32[10,64,4,4,64]{1,4,2,3,0:T(8,128)} %get-tuple-element.182), kind=kOutput, calls=%fused_computation.236 | convolution fusion | flops 511180800 | bytes 22489088 | tf_op jit(solution)/shard_map/btgik,ikd->btgd/dot_general | solution.py:164
  347.5 7.9 %fusion.123 = f32[10,64,4,128,1]{3,1,2,0,4:T(8,128)} fusion(bf16[8,12,2,64,128]{4,3,2,1,0:T(8,128)(2,1)} %bitcast.751, f32[10,64,4,12,64]{1,4,2,0,3:T(8,128)} %get-tuple-element.196, f32[10,64,4]{1,2,0:T(4,128)S(1)} %reduce_max.189, f32[10,64,4,4,64]{1,4,2,3,0:T(8,128)} %get-tuple-element.194), kind=kOutput, calls=%fused_computation.230 | convolution fusion | flops 511180800 | bytes 22489088 | tf_op jit(solution)/shard_map/btgik,ikd->btgd/dot_general | solution.py:164
  365.8 7.9 %fusion.120 = f32[10,64,4,128,1]{3,1,2,0,4:T(8,128)} fusion(bf16[8,12,2,64,128]{4,3,2,1,0:T(8,128)(2,1)} %bitcast.754, f32[10,64,4,12,64]{1,4,2,0,3:T(8,128)} %get-tuple-element.192, f32[10,64,4]{1,2,0:T(4,128)S(1)} %reduce_max.198, f32[10,64,4,4,64]{1,4,2,3,0:T(8,128)} %get-tuple-element.190), kind=kOutput, calls=%fused_computation.221 | convolution fusion | flops 511180800 | bytes 22489088 | tf_op jit(solution)/shard_map/btgik,ikd->btgd/dot_general | solution.py:164
  386.2 8.1 %multiply_reduce_fusion = (f32[80,64,4]{1,2,0:T(4,128)S(1)}, f32[80,64,4,64]{1,3,2,0:T(8,128)S(1)}) fusion(bf16[80,64,4,128]{3,1,2,0:T(8,128)(2,1)} %gather_fusion.2, bf16[80,2,64,128]{3,2,1,0:T(8,128)(2,1)} %gather_fusion.5), kind=kOutput, calls=%fused_computation.64 | convolution fusion | flops 338145280 | bytes 11878400 | tf_op jit(solution)/shard_map/...tgd,...kd->...tgk/dot_general | solution.py:18
  400.9 6.9 %divide_convert_fusion = bf16[80,64,4,128]{3,1,0,2:T(8,128)(2,1)S(1)} fusion(f32[80,64,4]{1,0,2:T(8,128)S(1)} %copy.306, bf16[80,64,4,64]{1,3,2,0:T(8,128)(2,1)} %get-tuple-element.75, bf16[80,2,64,128]{3,2,1,0:T(8,128)(2,1)} %gather_fusion.5), kind=kOutput, calls=%fused_computation.62 | convolution fusion | flops 340787200 | bytes 11878400 | tf_op jit(solution)/shard_map/...tgk,...kd->...tgd/dot_general | solution.py:24
  (419 shorter events, 219.1 us)
Async XLA Ops:
  6.5 20.2 %copy-start = (bf16[640,8,128]{2,1,0:T(8,128)(2,1)S(1)}, bf16[640,8,128]{2,1,0:T(8,128)(2,1)}, u32[]{:S(2)}) copy-start(bf16[640,8,128]{2,1,0:T(8,128)(2,1)} %param.8) | copy-start | bytes 3932164
  6.5 18.1 %copy-start.63 = (s32[8,1280]{1,0:T(8,128)S(1)}, s32[8,1280]{1,0:T(8,128)}, u32[]{:S(2)}) copy-start(s32[8,1280]{1,0:T(8,128)} %param.11) | copy-start | bytes 122884
  6.5 159.2 %all-gather.2.cloned.1.call-start = ((), (), s32[]{:S(2)}) async-start(), calls=%async_computation.1 | async-start | bytes 4227072 | tf_op jit(solution)/shard_map/all_gather | solution.py:84
  20.1 69.7 %collective-permute-start = (bf16[2,448,8,128]{3,2,1,0:T(8,128)(2,1)}, bf16[2,448,8,128]{3,2,1,0:T(8,128)(2,1)}, u32[]{:S(2)}, u32[]{:S(2)}) collective-permute-start(bf16[2,448,8,128]{3,2,1,0:T(8,128)(2,1)} %pad_maximum_fusion.2), channel_id=1, source_target_pairs={{0,1},{1,2},{2,3},{3,4},{4,5},{5,6},{6,7},{7,8},{8,9},{9,10},{10,1... | collective-permute-start | bytes 5505032 | tf_op jit(solution)/shard_map/ppermute | solution.py:13
  45.7 334.2 %all-to-all-start = ((bf16[128,2,2,64,128]{4,3,2,1,0:T(8,128)(2,1)}), bf16[128,2,2,64,128]{4,3,2,1,0:T(8,128)(2,1)}, u32[]{:S(2)}, u32[]{:S(2)}) async-start(bf16[128,2,2,64,128]{4,3,2,1,0:T(8,128)(2,1)} %maximum_select_fusion), calls=%async_computation | async-start | bytes 16777216 | tf_op jit(solution)/shard_map/all_to_all | solution.py:42
  109.3 13.1 %copy-start.17 = (bf16[17,64,128]{2,1,0:T(8,128)(2,1)S(1)}, bf16[17,64,128]{2,1,0:T(8,128)(2,1)}, u32[]{:S(2)}) copy-start(bf16[17,64,128]{2,1,0:T(8,128)(2,1)} %get-tuple-element.96) | copy-start | bytes 835588
  109.3 14.6 %copy-start.12 = (bf16[17,64,128]{2,1,0:T(8,128)(2,1)S(1)}, bf16[17,64,128]{2,1,0:T(8,128)(2,1)}, u32[]{:S(2)}) copy-start(bf16[17,64,128]{2,1,0:T(8,128)(2,1)} %get-tuple-element.89) | copy-start | bytes 835588
  109.3 16.1 %copy-start.16 = (bf16[17,64,128]{2,1,0:T(8,128)(2,1)S(1)}, bf16[17,64,128]{2,1,0:T(8,128)(2,1)}, u32[]{:S(2)}) copy-start(bf16[17,64,128]{2,1,0:T(8,128)(2,1)} %get-tuple-element.97) | copy-start | bytes 835588
  114.3 14.1 %copy-start.15 = (bf16[17,64,128]{2,1,0:T(8,128)(2,1)S(1)}, bf16[17,64,128]{2,1,0:T(8,128)(2,1)}, u32[]{:S(2)}) copy-start(bf16[17,64,128]{2,1,0:T(8,128)(2,1)} %get-tuple-element.98) | copy-start | bytes 835588
  174.8 17.9 %slice-start.30 = ((s8[5242880]{0:T(1024)(128)(4,1)}), s8[4194304]{0:T(1024)(128)(4,1)S(1)}, s32[]{:S(2)}) async-start(s8[5242880]{0:T(1024)(128)(4,1)} %bitcast.728), calls=%async_computation.32 | async-start | bytes 8388608
  192.7 22.4 %slice-start.28 = ((s8[5242880]{0:T(1024)(128)(4,1)}), s8[4194304]{0:T(1024)(128)(4,1)S(1)}, s32[]{:S(2)}) async-start(s8[5242880]{0:T(1024)(128)(4,1)} %bitcast.726), calls=%async_computation.30 | async-start | bytes 8388608
  215.1 22.7 %slice-start.26 = ((s8[5242880]{0:T(1024)(128)(4,1)}), s8[4194304]{0:T(1024)(128)(4,1)S(1)}, s32[]{:S(2)}) async-start(s8[5242880]{0:T(1024)(128)(4,1)} %bitcast.724), calls=%async_computation.28 | async-start | bytes 8388608
  237.8 21.8 %slice-start.24 = ((s8[5242880]{0:T(1024)(128)(4,1)}), s8[4194304]{0:T(1024)(128)(4,1)S(1)}, s32[]{:S(2)}) async-start(s8[5242880]{0:T(1024)(128)(4,1)} %bitcast.722), calls=%async_computation.26 | async-start | bytes 8388608
  259.6 19.6 %slice-start.22 = ((s8[5242880]{0:T(1024)(128)(4,1)}), s8[4194304]{0:T(1024)(128)(4,1)S(1)}, s32[]{:S(2)}) async-start(s8[5242880]{0:T(1024)(128)(4,1)} %bitcast.720), calls=%async_computation.24 | async-start | bytes 8388608
  279.3 20.1 %slice-start.20 = ((s8[5242880]{0:T(1024)(128)(4,1)}), s8[4194304]{0:T(1024)(128)(4,1)S(1)}, s32[]{:S(2)}) async-start(s8[5242880]{0:T(1024)(128)(4,1)} %bitcast.718), calls=%async_computation.22 | async-start | bytes 8388608
  291.6 24.0 %slice-start.16 = ((s8[5242880]{0:T(1024)(128)(4,1)}), s8[4194304]{0:T(1024)(128)(4,1)S(1)}, s32[]{:S(2)}) async-start(s8[5242880]{0:T(1024)(128)(4,1)} %bitcast.714), calls=%async_computation.18 | async-start | bytes 8388608
  299.4 16.2 %slice-start.17 = ((s8[5242880]{0:T(1024)(128)(4,1)}), s8[1048576]{0:T(1024)(128)(4,1)S(1)}, s32[]{:S(2)}) async-start(s8[5242880]{0:T(1024)(128)(4,1)} %bitcast.714), calls=%async_computation.19 | async-start | bytes 2097152
  342.6 12.8 %slice-start.4 = ((s8[15728640]{0:T(1024)(128)(4,1)}), s8[4194304]{0:T(1024)(128)(4,1)S(1)}, s32[]{:S(2)}) async-start(s8[15728640]{0:T(1024)(128)(4,1)} %bitcast.706), calls=%async_computation.6 | async-start | bytes 8388608
  342.6 12.8 %slice-start.5 = ((s8[15728640]{0:T(1024)(128)(4,1)}), s8[4194304]{0:T(1024)(128)(4,1)S(1)}, s32[]{:S(2)}) async-start(s8[15728640]{0:T(1024)(128)(4,1)} %bitcast.706), calls=%async_computation.7 | async-start | bytes 8388608
  347.5 13.5 %slice-start.8 = ((s8[15728640]{0:T(1024)(128)(4,1)}), s8[4194304]{0:T(1024)(128)(4,1)S(1)}, s32[]{:S(2)}) async-start(s8[15728640]{0:T(1024)(128)(4,1)} %bitcast.708), calls=%async_computation.10 | async-start | bytes 8388608
  347.5 13.5 %slice-start.9 = ((s8[15728640]{0:T(1024)(128)(4,1)}), s8[4194304]{0:T(1024)(128)(4,1)S(1)}, s32[]{:S(2)}) async-start(s8[15728640]{0:T(1024)(128)(4,1)} %bitcast.708), calls=%async_computation.11 | async-start | bytes 8388608
  361.0 12.7 %slice-start.12 = ((s8[15728640]{0:T(1024)(128)(4,1)}), s8[4194304]{0:T(1024)(128)(4,1)S(1)}, s32[]{:S(2)}) async-start(s8[15728640]{0:T(1024)(128)(4,1)} %bitcast.710), calls=%async_computation.14 | async-start | bytes 8388608
  361.0 12.7 %slice-start.13 = ((s8[15728640]{0:T(1024)(128)(4,1)}), s8[4194304]{0:T(1024)(128)(4,1)S(1)}, s32[]{:S(2)}) async-start(s8[15728640]{0:T(1024)(128)(4,1)} %bitcast.710), calls=%async_computation.15 | async-start | bytes 8388608
  361.0 12.7 %slice-start.18 = ((s8[5242880]{0:T(1024)(128)(4,1)}), s8[1048576]{0:T(1024)(128)(4,1)S(1)}, s32[]{:S(2)}) async-start(s8[5242880]{0:T(1024)(128)(4,1)} %bitcast.716), calls=%async_computation.20 | async-start | bytes 2097152
  (85 other events, 640.6 us)
Sparse Core Ops, SparseCore 0:
  17.3 138.2 all-gather.1
where the time goes:
time: 445 us; the launch traced here: 440 us
  matrix products  182 us (41%)
  other arithmetic  125 us (28%)
  local copies, waits for them, and re-layouts  97.4 us (22%)
  between operations  20 us (4%)
  starting transfers between devices  15.1 us (3%)
    reduce_sum x8, other arithmetic, shards(): weight_sum = jnp.sum(weights, axis=(3, 4))  64.6 us
    dot_general x8, matrix products, shards(): jnp.einsum('btgd,ikd->btgik', q_here, vert_keys, preferred_element_type=j...  63.8 us
    dot_general x8, matrix products, shards(): jnp.einsum('btgik,ikd->btgd', low_weights[:, :, :, near_count:], vert_val...  48.3 us
    dot_general x8, matrix products, shards(): jnp.einsum('btgd,bikd->btgik', q_here, near_keys, preferred_element_type=...  29.4 us
    dot_general x8, matrix products, shards(): jnp.einsum('btgik,bikd->btgd', low_weights[:, :, :, :near_count], near_va...  25.4 us
    unnamed x20, other arithmetic  16.1 us
    gather x8, local copies, waits for them, and re-layouts, shards(): near_keys = key_ext[:, :, kv_head][near_index]  14.2 us
    gather x8, local copies, waits for them, and re-layouts, shards(): near_vals = val_ext[:, :, kv_head][near_index]  14 us
  transfers between devices with their start and end apart: 3, of which 0 were waited for; matrix products, arithmetic and copies ran while one was open for 78% of the time, Pallas kernels for 0%

commit v1 on v0

v1 whole, which is shorter than its diff:
```python
import functools

import jax
import jax.numpy as jnp
from jax import lax
from jax.experimental import pallas as pl
from jax.experimental.pallas import tpu as pltpu
from jax.sharding import PartitionSpec as P

BS = 64
NW = 8
CAP = 2
AXES = ("blk", "grid")
MASKED = -1e30
LOG2E = 1.4426950408889634


def local_kernel(
    core_sm, slot_sm, off_sm, first_sm,
    q_ref, ko_ref, vo_ref, kh_ref, vh_ref, bias_ref, mine_hbm, other_hbm,
    out_ref, lse_ref,
    kx, vx, kv_buf, vv_buf, sems,
    *, heads, verts, blocks, group, near, scale,
):
    h = pl.program_id(0)
    halo = kh_ref.shape[1]
    own = ko_ref.shape[1]

    def fetch(head, buf):
        def from_pair(k_src, v_src):
            for i in range(verts):
                slot = slot_sm[head, i]
                rows = pl.ds(i * BS, BS)
                pltpu.make_async_copy(k_src.at[slot], kv_buf.at[buf, rows], sems.at[buf, 0]).start()
                pltpu.make_async_copy(v_src.at[slot], vv_buf.at[buf, rows], sems.at[buf, 1]).start()

        @pl.when(core_sm[0] == 0)
        def _():
            from_pair(mine_hbm, other_hbm)

        @pl.when(core_sm[0] != 0)
        def _():
            from_pair(other_hbm, mine_hbm)

    @pl.when(h == 0)
    def _():
        fetch(0, 0)

    @pl.when(h + 1 < heads)
    def _():
        fetch(h + 1, (h + 1) % 2)

    kx[0:halo] = kh_ref[0]
    kx[halo : halo + own] = ko_ref[0]
    vx[0:halo] = vh_ref[0]
    vx[halo : halo + own] = vo_ref[0]
    cur = h % 2
    pltpu.make_async_copy(kv_buf.at[cur], kv_buf.at[cur], sems.at[cur, 0]).wait()
    pltpu.make_async_copy(vv_buf.at[cur], vv_buf.at[cur], sems.at[cur, 1]).wait()

    t_pos = lax.broadcasted_iota(jnp.int32, (BS, near * BS), 0)
    u_pos = lax.broadcasted_iota(jnp.int32, (BS, near * BS), 1)
    causal_bias = jnp.where((u_pos < BS) & (u_pos > t_pos), MASKED, 0.0)
    lane = lax.broadcasted_iota(jnp.int32, (1, near * BS), 1) // BS

    def one_block(b, carry):
        rows = pl.multiple_of(b * BS, BS)
        q = q_ref[0, :, pl.ds(rows, BS), :].reshape(group * BS, q_ref.shape[3])
        k_parts = []
        v_parts = []
        row_bias = jnp.zeros((1, near * BS), jnp.float32)
        for i in range(near):
            off = off_sm[h, i]
            start = pl.multiple_of((b + NW - 1 - off) * BS, BS)
            k_parts.append(kx[pl.ds(start, BS), :])
            v_parts.append(vx[pl.ds(start, BS), :])
            miss = jnp.where(first_sm[0] + b < off, MASKED, 0.0)
            row_bias = jnp.where(lane == i, miss, row_bias)
        k_near = jnp.concatenate(k_parts, axis=0)
        v_near = jnp.concatenate(v_parts, axis=0)
        dims = (((1,), (1,)), ((), ()))
        s_near = lax.dot_general(q, k_near, dims, preferred_element_type=jnp.float32)
        near_bias = causal_bias + row_bias
        s_near = (s_near.reshape(group, BS, near * BS) + near_bias[None]).reshape(s_near.shape)
        s_vert = lax.dot_general(q, kv_buf[cur], dims, preferred_element_type=jnp.float32)
        s_vert = s_vert + bias_ref[0, pl.ds(b, 1), :]
        top = jnp.maximum(
            jnp.max(s_near, axis=1, keepdims=True), jnp.max(s_vert, axis=1, keepdims=True)
        )
        p_near = jnp.exp2((s_near - top) * (scale * LOG2E))
        p_vert = jnp.exp2((s_vert - top) * (scale * LOG2E))
        total = jnp.sum(p_near, axis=1, keepdims=True) + jnp.sum(p_vert, axis=1, keepdims=True)
        acc = jnp.dot(p_near.astype(jnp.bfloat16), v_near, preferred_element_type=jnp.float32)
        acc = acc + jnp.dot(
            p_vert.astype(jnp.bfloat16), vv_buf[cur], preferred_element_type=jnp.float32
        )
        out_ref[0, b] = acc / total
        lse = top * scale + jnp.log(total)
        wide = jnp.broadcast_to(lse, (lse.shape[0], 128))
        lse_ref[0, b] = wide.T[0:1, :]
        return carry

    lax.fori_loop(0, blocks, one_block, 0)


def merge_kernel(
    slot_sm, valid_sm,
    q_ref, local_ref, lse_ref, far_hbm,
    out_ref,
    kv_buf, wide_out, sems,
    *, heads, blocks, group, scale,
):
    b = pl.program_id(0)

    def fetch(block, buf):
        for h in range(heads):
            slot = slot_sm[h * blocks + block]
            pltpu.make_async_copy(far_hbm.at[slot], kv_buf.at[buf, h], sems.at[buf]).start()

    @pl.when(b == 0)
    def _():
        fetch(0, 0)

    @pl.when(b + 1 < blocks)
    def _():
        fetch(b + 1, (b + 1) % 2)

    cur = b % 2
    pltpu.make_async_copy(kv_buf.at[cur], kv_buf.at[cur], sems.at[cur]).wait()
    rows = group * BS
    for h in range(heads):
        q = q_ref[h].reshape(rows, q_ref.shape[3])
        s = lax.dot_general(
            q, kv_buf[cur, h, 0], (((1,), (1,)), ((), ())), preferred_element_type=jnp.float32
        )
        top = jnp.max(s, axis=1, keepdims=True)
        p = jnp.exp2((s - top) * (scale * LOG2E))
        total = jnp.sum(p, axis=1, keepdims=True)
        acc = jnp.dot(
            p.astype(jnp.bfloat16), kv_buf[cur, h, 1], preferred_element_type=jnp.float32
        )
        far_out = (acc / total).astype(jnp.bfloat16).astype(jnp.float32)
        far_lse = top * scale + jnp.log(total)
        local_out = local_ref[h, 0]
        local_lse = jnp.broadcast_to(lse_ref[h, 0], (128, rows)).T
        joint = jnp.maximum(local_lse, far_lse)
        a = jnp.exp(local_lse - joint)
        c = jnp.exp(far_lse - joint)
        merged = (a * local_out + c * far_out) / (a + c)
        ok = valid_sm[h * blocks + b] > 0
        merged = jnp.where(ok, merged, local_out)
        for g in range(group):
            wide_out[pl.ds(h * group + g, BS, stride=heads * group), :] = merged[
                g * BS : (g + 1) * BS
            ]
    out_ref[...] = wide_out[...].reshape(out_ref.shape).astype(jnp.bfloat16)


def shards(queries, keys, values, vert_blocks, slash_offsets, far_blocks):
    tok, q_heads, dh = queries.shape
    heads = keys.shape[1]
    group = q_heads // heads
    blocks = tok // BS
    verts = vert_blocks.shape[1]
    near = slash_offsets.shape[1]
    reqs = heads * blocks
    devices = lax.axis_size(AXES)
    rank = lax.axis_index(AXES)
    core = rank % 2
    scale = dh**-0.5
    halo_rows = (NW - 1) * BS
    rows = group * BS

    vert_flat = vert_blocks.reshape(-1)
    is_mine = vert_flat // blocks == rank
    pick = jnp.max(jnp.where(is_mine, jnp.arange(heads * verts), 0))
    pick_head = pick // verts
    pick_row = jnp.clip(jnp.max(jnp.where(is_mine, vert_flat - rank * blocks, 0)), 0, blocks - 1) * BS
    v_key = lax.dynamic_slice(keys, (pick_row, pick_head, 0), (BS, 1, dh)).reshape(1, 1, BS, dh)
    v_val = lax.dynamic_slice(values, (pick_row, pick_head, 0), (BS, 1, dh)).reshape(1, 1, BS, dh)
    vert_send = jnp.broadcast_to(
        jnp.concatenate([v_key, v_val], axis=1), (devices // 2, 2, BS, dh)
    ).reshape(devices, BS, dh)
    vert_mine = lax.all_to_all(vert_send, AXES, split_axis=0, concat_axis=0, tiled=True)

    k_t = keys.transpose(1, 0, 2)
    v_t = values.transpose(1, 0, 2)
    rim = jnp.stack([k_t[:, tok - halo_rows :], v_t[:, tok - halo_rows :]])
    before = lax.ppermute(rim, AXES, [(i, i + 1) for i in range(devices - 1)])

    all_far = far_blocks.reshape(heads, devices, blocks).transpose(1, 0, 2).reshape(devices, reqs)
    earlier = (jnp.arange(reqs)[:, None] < jnp.arange(reqs)[None, :]).astype(jnp.float32)
    asked = (all_far >= 0) & (all_far // blocks == rank)
    place = jnp.dot(asked.astype(jnp.float32), earlier).astype(jnp.int32)
    tile = (jnp.arange(reqs)[None, :] // blocks) * blocks + all_far - rank * blocks
    wanted = asked[:, None, :] & (place[:, None, :] == jnp.arange(CAP)[None, :, None])
    send_tile = jnp.max(jnp.where(wanted, tile[:, None, :], 0), axis=2).reshape(-1)
    tiles = jnp.stack(
        [k_t.reshape(heads * blocks, BS, dh), v_t.reshape(heads * blocks, BS, dh)], axis=1
    )
    far_send = tiles[send_tile]
    far_send, vert_mine = lax.optimization_barrier((far_send, vert_mine))
    vert_other = lax.ppermute(vert_mine, AXES, [(i, i ^ 1) for i in range(devices)])
    far_got = lax.all_to_all(far_send, AXES, split_axis=0, concat_axis=0, tiled=True)

    my_far = lax.dynamic_slice_in_dim(far_blocks, rank * blocks, blocks, 1).reshape(-1)
    valid = (my_far >= 0).astype(jnp.int32)
    owner = jnp.where(my_far >= 0, my_far // blocks, -1)
    same = owner[:, None] == owner[None, :]
    my_place = jnp.sum(same & (jnp.arange(reqs)[None, :] < jnp.arange(reqs)[:, None]), axis=1)
    got_slot = jnp.where(my_far >= 0, owner * CAP + jnp.minimum(my_place, CAP - 1), 0)

    q_t = queries.reshape(tok, heads, group, dh).transpose(1, 2, 0, 3)
    zero_at = jnp.argmax((slash_offsets == 0).astype(jnp.int32), axis=1)
    order = (zero_at[:, None] + jnp.arange(near)[None, :]) % near
    offsets = jnp.sum(
        jnp.where(order[:, :, None] == jnp.arange(near)[None, None, :], slash_offsets[:, None, :], 0),
        axis=2,
    )
    my_blocks = rank * blocks + jnp.arange(blocks)
    vert_ok = vert_blocks[:, None, :] <= my_blocks[None, :, None] - NW
    vert_bias = jnp.repeat(jnp.where(vert_ok, 0.0, MASKED).astype(jnp.float32), BS, axis=2)

    by_head = lambda *tail: pl.BlockSpec((1,) + tail, lambda h, *_: (h,) + (0,) * len(tail))
    local_out, local_lse = pl.pallas_call(
        functools.partial(
            local_kernel, heads=heads, verts=verts, blocks=blocks, group=group, near=near,
            scale=scale,
        ),
        grid_spec=pltpu.PrefetchScalarGridSpec(
            num_scalar_prefetch=4,
            grid=(heads,),
            in_specs=[
                by_head(group, tok, dh),
                by_head(tok, dh),
                by_head(tok, dh),
                by_head(halo_rows, dh),
                by_head(halo_rows, dh),
                by_head(blocks, verts * BS),
                pl.BlockSpec(memory_space=pl.ANY),
                pl.BlockSpec(memory_space=pl.ANY),
            ],
            out_specs=[by_head(blocks, rows, dh), by_head(blocks, 1, rows)],
            scratch_shapes=[
                pltpu.VMEM((halo_rows + tok, dh), jnp.bfloat16),
                pltpu.VMEM((halo_rows + tok, dh), jnp.bfloat16),
                pltpu.VMEM((2, verts * BS, dh), jnp.bfloat16),
                pltpu.VMEM((2, verts * BS, dh), jnp.bfloat16),
                pltpu.SemaphoreType.DMA((2, 2)),
            ],
        ),
        out_shape=[
            jax.ShapeDtypeStruct((heads, blocks, rows, dh), jnp.float32),
            jax.ShapeDtypeStruct((heads, blocks, 1, rows), jnp.float32),
        ],
        compiler_params=pltpu.CompilerParams(vmem_limit_bytes=40 * 1024 * 1024),
        cost_estimate=pl.CostEstimate(
            flops=4 * heads * blocks * rows * dh * (near + verts) * BS,
            bytes_accessed=40_000_000,
            transcendentals=heads * blocks * rows * (near + verts) * BS,
        ),
        name="local_attention",
    )(
        core.reshape(1).astype(jnp.int32),
        (vert_blocks // blocks).astype(jnp.int32),
        offsets.astype(jnp.int32),
        (rank * blocks).reshape(1).astype(jnp.int32),
        q_t, k_t, v_t, before[0], before[1], vert_bias, vert_mine, vert_other,
    )

    attended = pl.pallas_call(
        functools.partial(merge_kernel, heads=heads, blocks=blocks, group=group, scale=scale),
        grid_spec=pltpu.PrefetchScalarGridSpec(
            num_scalar_prefetch=2,
            grid=(blocks,),
            in_specs=[
                pl.BlockSpec((heads, group, BS, dh), lambda b, *_: (0, 0, b, 0)),
                pl.BlockSpec((heads, 1, rows, dh), lambda b, *_: (0, b, 0, 0)),
                pl.BlockSpec((heads, 1, 1, rows), lambda b, *_: (0, b, 0, 0)),
                pl.BlockSpec(memory_space=pl.ANY),
            ],
            out_specs=pl.BlockSpec((BS, q_heads, dh), lambda b, *_: (b, 0, 0)),
            scratch_shapes=[
                pltpu.VMEM((2, heads, 2, BS, dh), jnp.bfloat16),
                pltpu.VMEM((BS * q_heads, dh), jnp.float32),
                pltpu.SemaphoreType.DMA((2,)),
            ],
        ),
        out_shape=jax.ShapeDtypeStruct((tok, q_heads, dh), jnp.bfloat16),
        compiler_params=pltpu.CompilerParams(vmem_limit_bytes=40 * 1024 * 1024),
        cost_estimate=pl.CostEstimate(
            flops=4 * heads * blocks * rows * dh * BS,
            bytes_accessed=25_000_000,
            transcendentals=heads * blocks * rows * BS,
        ),
        name="far_merge",
    )(got_slot.astype(jnp.int32), valid, q_t, local_out, local_lse, far_got)
    return attended


def solution(mesh):
    split = P(AXES, None, None)
    return jax.shard_map(
        shards,
        mesh=mesh,
        in_specs=(split, split, split, P(), P(), P()),
        out_specs=split,
        check_vma=False,
    )
```

time: 445 us -> 263 us (0.59)
  the two profiles are of different devices: /device:TPU:1 before, /device:TPU:82 now
where the time goes in v1:
time: 263 us; the launch traced here: 262 us
  waiting for transfers between devices  116 us (44%)
  Pallas kernels  79.6 us (30%)
  local copies, waits for them, and re-layouts  29.2 us (11%)
  starting transfers between devices  25.5 us (10%)
  other arithmetic  7.83 us (3%)
  between operations  3.07 us (1%)
    ppermute x1, waiting for transfers between devices, shards(): before = lax.ppermute(rim, AXES, [(i, i + 1) for i in range(devices - 1)])  105 us
    pallas_call x1, Pallas kernels, shards(): pl.pallas_call(functools.partial(local_kernel, heads=heads, verts=verts,...  56.3 us
    pallas_call x1, Pallas kernels, shards(): pl.pallas_call(functools.partial(merge_kernel, heads=heads, blocks=blocks...  23.3 us
    unnamed x15, local copies, waits for them, and re-layouts  13.7 us
    all_to_all x1, starting transfers between devices, shards(): lax.all_to_all(far_send, AXES, split_axis=0, concat_axis=0, tiled=True)  11.4 us
    all_to_all x1, waiting for transfers between devices, shards(): lax.all_to_all(vert_send, AXES, split_axis=0, concat_axis=0, tiled=True)  11.2 us
    all_to_all x1, starting transfers between devices, shards(): lax.all_to_all(vert_send, AXES, split_axis=0, concat_axis=0, tiled=True)  10.4 us
    gather x1, local copies, waits for them, and re-layouts, shards(): far_send = tiles[send_tile]  10.2 us
  transfers between devices with their start and end apart: 4, of which 2 were waited for; matrix products, arithmetic and copies ran while one was open for 10% of the time, Pallas kernels for 22%

profile of v1, /device:TPU:82, one launch (start us, length us, event | category | flops | bytes accessed | tf_op | source)
XLA Modules:
  0.0 261.7 jit_solution(11957596082965130342)
XLA Ops:
  0.0 0.7 broadcast_compare_fusion
  0.7 1.4 select_reduce_fusion.2
  4.8 1.6 copy.38
  6.7 1.8 broadcast_in_dim.75
  8.5 10.4 %all-to-all-start = ((bf16[128,64,128]{2,1,0:T(8,128)(2,1)}), bf16[128,64,128]{2,1,0:T(8,128)(2,1)}, u32[]{:S(2)}, u32[]{:S(2)}) async-start(bf16[128,64,128]{2,1,0:T(8,128)(2,1)} %bitcast.43), calls=%async_computation | async-start | bytes 4194304 | tf_op jit(solution)/shard_map/all_to_all | solution.py:184
  18.9 0.5 reshape.230
  20.3 1.7 pad_maximum_fusion
  22.0 10.2 %gather_fusion = bf16[256,2,64,128]{3,2,1,0:T(8,128)(2,1)} fusion(bf16[80,2,64,128]{3,2,0,1:T(8,128)(2,1)} %pad_maximum_fusion, s32[1024]{0:T(1024)S(1)} %pad_clamp_fusion), kind=kCustom, calls=%fused_computation | custom fusion | bytes 16778240 | tf_op jit(solution)/shard_map/gather | solution.py:201
  32.2 11.2 %all-to-all-done.mine_hbm = bf16[128,64,128]{2,1,0:T(8,128)(2,1)} async-done(((bf16[128,64,128]{2,1,0:T(8,128)(2,1)}), bf16[128,64,128]{2,1,0:T(8,128)(2,1)}, u32[]{:S(2)}, u32[]{:S(2)}) %all-to-all-start) | async-done | bytes 2097184 | tf_op jit(solution)/shard_map/all_to_all | solution.py:184
  43.4 11.4 %all-to-all-start.1 = ((bf16[256,2,64,128]{3,2,1,0:T(8,128)(2,1)}), bf16[256,2,64,128]{3,2,1,0:T(8,128)(2,1)}, u32[]{:S(2)}, u32[]{:S(2)}) async-start(bf16[256,2,64,128]{3,2,1,0:T(8,128)(2,1)} %gather_fusion), calls=%async_computation.1 | async-start | bytes 16777216 | tf_op jit(solution)/shard_map/all_to_all | solution.py:204
  55.0 1.4 pad_maximum_fusion.1
  56.4 2.0 collective-permute-start
  58.4 1.7 collective-permute-start.1
  60.2 0.2 broadcast_in_dim.71
  60.7 6.9 %copy.25 = bf16[640,32,128]{2,0,1:T(8,128)(2,1)} copy(bf16[640,32,128]{2,1,0:T(8,128)(2,1)} %param.6) | data formatting | bytes 10485760 | tf_op args[0]
  67.6 0.5 iota_reduce_fusion
  68.3 0.8 fusion.4
  69.2 0.8 dynamic-slice_divide_fusion
  70.3 105.0 %collective-permute-done = bf16[2,8,448,128]{3,2,1,0:T(8,128)(2,1)} collective-permute-done((bf16[2,8,448,128]{3,2,1,0:T(8,128)(2,1)}, bf16[2,8,448,128]{3,2,1,0:T(8,128)(2,1)}, u32[]{:S(2)}, u32[]{:S(2)}) %collective-permute-start) | collective-permute-done | bytes 1835040 | tf_op jit(solution)/shard_map/ppermute | solution.py:189
  175.3 1.6 slice_bitcast_fusion
  176.9 2.5 copy-done
  179.4 56.3 %local_attention.1 = (f32[8,10,256,128]{3,2,1,0:T(8,128)}, f32[8,10,1,256]{3,2,1,0:T(1,128)S(1)}) custom-call(s32[1]{0:T(128)} %bitcast.2.core_sm, s32[8,12]{1,0:T(8,128)S(1)} %get-tuple-element.18.slot_sm, s32[8,4]{1,0:T(8,128)S(1)} %copy.32.off_sm, s32[1]{0:T(128)} %bitcast.3.first_sm, bf16[8,4,640,128]{3,2,1,0:T(8,128)(2,1)S(1)} %bitcast.35, ...), custom_call_target="tpu_custom_call" | custom-call | flops 10737418240 | bytes 40000000 | tf_op jit(solution)/shard_map/local_attention/pallas_call | solution.py:225
  235.7 2.5 copy-done.1
  238.2 23.3 %far_merge.1 = bf16[640,32,128]{2,1,0:T(8,128)(2,1)} custom-call(s32[80]{0:T(128)S(1)} %add_select_fusion.4.slot_sm, s32[80]{0:T(128)S(1)} %convert_element_type.15.valid_sm, bf16[8,4,640,128]{3,2,1,0:T(8,128)(2,1)S(1)} %bitcast.36, f32[8,10,256,128]{3,2,1,0:T(8,128)} %get-tuple-element.12.local_ref, f32[8,10,1,256]{3,2,1,0:T(1,128)S(1)} %get-tuple-element.13.lse_ref, ...), custom_call_target="tpu_custom_call" | custom-call | flops 671088640 | bytes 25000000 | tf_op jit(solution)/shard_map/far_merge/pallas_call | solution.py:271
  (41 shorter events, 2.2 us)
Async XLA Ops:
  4.8 1.7 copy-start.2
  8.5 10.4 %copy-start.3 = (s32[8,1280]{1,0:T(8,128)S(1)}, s32[8,1280]{1,0:T(8,128)}, u32[]{:S(2)}) copy-start(s32[8,1280]{1,0:T(8,128)} %param.11) | copy-start | bytes 122884
  8.5 34.9 %all-to-all-start = ((bf16[128,64,128]{2,1,0:T(8,128)(2,1)}), bf16[128,64,128]{2,1,0:T(8,128)(2,1)}, u32[]{:S(2)}, u32[]{:S(2)}) async-start(bf16[128,64,128]{2,1,0:T(8,128)(2,1)} %bitcast.43), calls=%async_computation | async-start | bytes 4194304 | tf_op jit(solution)/shard_map/all_to_all | solution.py:184
  43.4 192.2 %all-to-all-start.1 = ((bf16[256,2,64,128]{3,2,1,0:T(8,128)(2,1)}), bf16[256,2,64,128]{3,2,1,0:T(8,128)(2,1)}, u32[]{:S(2)}, u32[]{:S(2)}) async-start(bf16[256,2,64,128]{3,2,1,0:T(8,128)(2,1)} %gather_fusion), calls=%async_computation.1 | async-start | bytes 16777216 | tf_op jit(solution)/shard_map/all_to_all | solution.py:204
  55.0 5.2 %copy-start.4 = (s32[8,12]{1,0:T(8,128)S(1)}, s32[8,12]{1,0:T(8,128)}, u32[]{:S(2)}) copy-start(s32[8,12]{1,0:T(8,128)} %param.9) | copy-start | bytes 1156
  56.4 118.9 %collective-permute-start = (bf16[2,8,448,128]{3,2,1,0:T(8,128)(2,1)}, bf16[2,8,448,128]{3,2,1,0:T(8,128)(2,1)}, u32[]{:S(2)}, u32[]{:S(2)}) collective-permute-start(bf16[2,8,448,128]{3,2,1,0:T(8,128)(2,1)} %pad_maximum_fusion.1), channel_id=1, source_target_pairs={{0,1},{1,2},{2,3},{3,4},{4,5},{5,6},{6,7},{7,8},{8,9},{9,10},{10,1... | collective-permute-start | bytes 5505032 | tf_op jit(solution)/shard_map/ppermute | solution.py:189
  58.4 118.4 %collective-permute-start.1 = (bf16[128,64,128]{2,1,0:T(8,128)(2,1)}, bf16[128,64,128]{2,1,0:T(8,128)(2,1)}, u32[]{:S(2)}, u32[]{:S(2)}) collective-permute-start(bf16[128,64,128]{2,1,0:T(8,128)(2,1)} %all-to-all-done.mine_hbm), channel_id=1, source_target_pairs={{0,1},{1,0},{2,3},{3,2},{4,5},{5,4},{6,7},{7,6},{8,9},{9,8},{10,11... | collective-permute-start | bytes 6291464 | tf_op jit(solution)/shard_map/ppermute | solution.py:203
  60.7 6.9 %copy-start.5 = (s32[8,4]{0,1:T(4,128)S(1)}, s32[8,4]{0,1:T(4,128)}, u32[]{:S(2)}) copy-start(s32[8,4]{0,1:T(4,128)} %param.10) | copy-start | bytes 388
  176.9 2.5 copy-start
  235.7 2.5 copy-start.1

commit v2 on v1

--- a/solution.py
+++ b/solution.py
@@ -58,14 +58,14 @@
     pltpu.make_async_copy(kv_buf.at[cur], kv_buf.at[cur], sems.at[cur, 0]).wait()
     pltpu.make_async_copy(vv_buf.at[cur], vv_buf.at[cur], sems.at[cur, 1]).wait()
 
-    t_pos = lax.broadcasted_iota(jnp.int32, (BS, near * BS), 0)
-    u_pos = lax.broadcasted_iota(jnp.int32, (BS, near * BS), 1)
+    t_pos = lax.broadcasted_iota(jnp.int32, (group * BS, near * BS), 0) // group
+    u_pos = lax.broadcasted_iota(jnp.int32, (group * BS, near * BS), 1)
     causal_bias = jnp.where((u_pos < BS) & (u_pos > t_pos), MASKED, 0.0)
     lane = lax.broadcasted_iota(jnp.int32, (1, near * BS), 1) // BS
 
     def one_block(b, carry):
-        rows = pl.multiple_of(b * BS, BS)
-        q = q_ref[0, :, pl.ds(rows, BS), :].reshape(group * BS, q_ref.shape[3])
+        rows = pl.multiple_of(b * group * BS, group * BS)
+        q = q_ref[0, pl.ds(rows, group * BS), :]
         k_parts = []
         v_parts = []
         row_bias = jnp.zeros((1, near * BS), jnp.float32)
@@ -80,8 +80,7 @@
         v_near = jnp.concatenate(v_parts, axis=0)
         dims = (((1,), (1,)), ((), ()))
         s_near = lax.dot_general(q, k_near, dims, preferred_element_type=jnp.float32)
-        near_bias = causal_bias + row_bias
-        s_near = (s_near.reshape(group, BS, near * BS) + near_bias[None]).reshape(s_near.shape)
+        s_near = s_near + (causal_bias + row_bias)
         s_vert = lax.dot_general(q, kv_buf[cur], dims, preferred_element_type=jnp.float32)
         s_vert = s_vert + bias_ref[0, pl.ds(b, 1), :]
         top = jnp.maximum(
@@ -96,8 +95,7 @@
         )
         out_ref[0, b] = acc / total
         lse = top * scale + jnp.log(total)
-        wide = jnp.broadcast_to(lse, (lse.shape[0], 128))
-        lse_ref[0, b] = wide.T[0:1, :]
+        lse_ref[0, pl.ds(b, 1), :] = jnp.broadcast_to(lse, (lse.shape[0], 128)).T[0:1, :]
         return carry
 
     lax.fori_loop(0, blocks, one_block, 0)
@@ -107,7 +105,7 @@
     slot_sm, valid_sm,
     q_ref, local_ref, lse_ref, far_hbm,
     out_ref,
-    kv_buf, wide_out, sems,
+    kv_buf, sems,
     *, heads, blocks, group, scale,
 ):
     b = pl.program_id(0)
@@ -128,32 +126,94 @@
     cur = b % 2
     pltpu.make_async_copy(kv_buf.at[cur], kv_buf.at[cur], sems.at[cur]).wait()
     rows = group * BS
+    dh = q_ref.shape[2]
+    weights = []
+    tops = []
+    totals = []
     for h in range(heads):
-        q = q_ref[h].reshape(rows, q_ref.shape[3])
         s = lax.dot_general(
-            q, kv_buf[cur, h, 0], (((1,), (1,)), ((), ())), preferred_element_type=jnp.float32
+            kv_buf[cur, h, 0], q_ref[h], (((1,), (1,)), ((), ())),
+            preferred_element_type=jnp.float32,
         )
-        top = jnp.max(s, axis=1, keepdims=True)
+        top = jnp.max(s, axis=0, keepdims=True)
         p = jnp.exp2((s - top) * (scale * LOG2E))
-        total = jnp.sum(p, axis=1, keepdims=True)
-        acc = jnp.dot(
-            p.astype(jnp.bfloat16), kv_buf[cur, h, 1], preferred_element_type=jnp.float32
+        weights.append(p)
+        tops.append(top)
+        totals.append(jnp.sum(p, axis=0, keepdims=True))
+    total = jnp.concatenate(totals, axis=0)
+    far_lse = jnp.concatenate(tops, axis=0) * scale + jnp.log(total)
+    local_lse = lse_ref[0]
+    joint = jnp.maximum(local_lse, far_lse)
+    head_row = lax.broadcasted_iota(jnp.int32, (heads, 1), 0)
+    valid = jnp.zeros((heads, 1), jnp.int32)
+    for h in range(heads):
+        valid = jnp.where(head_row == h, valid_sm[h * blocks + b], valid)
+    a = jnp.where(valid > 0, jnp.exp(local_lse - joint), 1.0)
+    c = jnp.where(valid > 0, jnp.exp(far_lse - joint), 0.0)
+    local_share = (a / (a + c)).T
+    far_share = c / ((a + c) * total)
+
+    low = lax.broadcasted_iota(jnp.int32, (rows // 8, 8, dh), 1) < group
+    for quad in range(heads // 4):
+        wide = []
+        for pair in (2 * quad, 2 * quad + 1):
+            halves = []
+            for h in (2 * pair, 2 * pair + 1):
+                p = (weights[h] * far_share[h : h + 1]).astype(jnp.bfloat16)
+                acc = lax.dot_general(
+                    p, kv_buf[cur, h, 1], (((0,), (0,)), ((), ())),
+                    preferred_element_type=jnp.float32,
+                )
+                mixed = local_share[:, h : h + 1] * local_ref[h, 0] + acc
+                halves.append(mixed.reshape(rows // 8, 8, dh))
+            x, y = halves
+            even = jnp.where(low, x, pltpu.roll(y, group, 1))
+            odd = jnp.where(low, pltpu.roll(x, group, 1), y)
+            wide.append(jnp.stack([even, odd], axis=1).reshape(BS, 8, dh))
+        both = jnp.concatenate(wide, axis=1)
+        out_ref[:, quad * 16 : (quad + 1) * 16, :] = both.astype(jnp.bfloat16)
+
+
+def vert_pack_kernel(
+    rank_sm, vert_sm,
+    keys_hbm, values_hbm,
+    out_hbm,
+    tok_buf, send_buf, sems,
+    *, count, verts, blocks, copies,
+):
+    def look(i, carry):
+        head, block = carry
+        at = vert_sm[i]
+        mine = at // blocks == rank_sm[0]
+        return (
+            jnp.where(mine, i // verts, head),
+            jnp.where(mine, at - rank_sm[0] * blocks, block),
         )
-        far_out = (acc / total).astype(jnp.bfloat16).astype(jnp.float32)
-        far_lse = top * scale + jnp.log(total)
-        local_out = local_ref[h, 0]
-        local_lse = jnp.broadcast_to(lse_ref[h, 0], (128, rows)).T
-        joint = jnp.maximum(local_lse, far_lse)
-        a = jnp.exp(local_lse - joint)
-        c = jnp.exp(far_lse - joint)
-        merged = (a * local_out + c * far_out) / (a + c)
-        ok = valid_sm[h * blocks + b] > 0
-        merged = jnp.where(ok, merged, local_out)
-        for g in range(group):
-            wide_out[pl.ds(h * group + g, BS, stride=heads * group), :] = merged[
-                g * BS : (g + 1) * BS
-            ]
-    out_ref[...] = wide_out[...].reshape(out_ref.shape).astype(jnp.bfloat16)
+
+    head, block = lax.fori_loop(0, count, look, (jnp.int32(0), jnp.int32(0)))
+    rows = pl.ds(pl.multiple_of(block * BS, BS), BS)
+    loads = [
+        pltpu.make_async_copy(keys_hbm.at[rows], tok_buf.at[0], sems.at[0]),
+        pltpu.make_async_copy(values_hbm.at[rows], tok_buf.at[1], sems.at[1]),
+    ]
+    for load in loads:
+        load.start()
+    for which, load in enumerate(loads):
+        load.wait()
+        tokens = tok_buf[which].astype(jnp.float32)
+        here = lax.broadcasted_iota(jnp.int32, tokens.shape, 1) == head
+        tile = jnp.sum(jnp.where(here, tokens, 0.0), axis=1).astype(jnp.bfloat16)
+        for i in range(which, send_buf.shape[0], 2):
+            send_buf[i] = tile
+    chunk = send_buf.shape[0]
+    stores = [
+        pltpu.make_async_copy(send_buf, out_hbm.at[pl.ds(i * chunk, chunk)], sems.at[2 + i])
+        for i in range(copies)
+    ]
+    for store in stores:
+        store.start()
+    for store in stores:
+        store.wait()
 
 
 def shards(queries, keys, values, vert_blocks, slash_offsets, far_blocks):
@@ -171,22 +231,34 @@
     halo_rows = (NW - 1) * BS
     rows = group * BS
 
-    vert_flat = vert_blocks.reshape(-1)
-    is_mine = vert_flat // blocks == rank
-    pick = jnp.max(jnp.where(is_mine, jnp.arange(heads * verts), 0))
-    pick_head = pick // verts
-    pick_row = jnp.clip(jnp.max(jnp.where(is_mine, vert_flat - rank * blocks, 0)), 0, blocks - 1) * BS
-    v_key = lax.dynamic_slice(keys, (pick_row, pick_head, 0), (BS, 1, dh)).reshape(1, 1, BS, dh)
-    v_val = lax.dynamic_slice(values, (pick_row, pick_head, 0), (BS, 1, dh)).reshape(1, 1, BS, dh)
-    vert_send = jnp.broadcast_to(
-        jnp.concatenate([v_key, v_val], axis=1), (devices // 2, 2, BS, dh)
-    ).reshape(devices, BS, dh)
+    forward = [(i, i + 1) for i in range(devices - 1)]
+    halo_k = lax.ppermute(keys[tok - halo_rows :], AXES, forward)
+    halo_v = lax.ppermute(values[tok - halo_rows :], AXES, forward)
+
+    copies = 8
+    vert_send = pl.pallas_call(
+        functools.partial(
+            vert_pack_kernel, count=heads * verts, verts=verts, blocks=blocks, copies=copies
+        ),
+        grid_spec=pltpu.PrefetchScalarGridSpec(
+            num_scalar_prefetch=2,
+            grid=(1,),
+            in_specs=[pl.BlockSpec(memory_space=pl.ANY), pl.BlockSpec(memory_space=pl.ANY)],
+            out_specs=pl.BlockSpec(memory_space=pl.ANY),
+            scratch_shapes=[
+                pltpu.VMEM((2, BS, heads, dh), jnp.bfloat16),
+                pltpu.VMEM((devices // copies, BS, dh), jnp.bfloat16),
+                pltpu.SemaphoreType.DMA((2 + copies,)),
+            ],
+        ),
+        out_shape=jax.ShapeDtypeStruct((devices, BS, dh), jnp.bfloat16),
+        name="vertical_pack",
+    )(rank.reshape(1).astype(jnp.int32), vert_blocks.reshape(-1), keys, values)
+    vert_send, halo_k = lax.optimization_barrier((vert_send, halo_k))
     vert_mine = lax.all_to_all(vert_send, AXES, split_axis=0, concat_axis=0, tiled=True)
 
     k_t = keys.transpose(1, 0, 2)
     v_t = values.transpose(1, 0, 2)
-    rim = jnp.stack([k_t[:, tok - halo_rows :], v_t[:, tok - halo_rows :]])
-    before = lax.ppermute(rim, AXES, [(i, i + 1) for i in range(devices - 1)])
 
     all_far = far_blocks.reshape(heads, devices, blocks).transpose(1, 0, 2).reshape(devices, reqs)
     earlier = (jnp.arange(reqs)[:, None] < jnp.arange(reqs)[None, :]).astype(jnp.float32)
@@ -199,8 +271,11 @@
         [k_t.reshape(heads * blocks, BS, dh), v_t.reshape(heads * blocks, BS, dh)], axis=1
     )
     far_send = tiles[send_tile]
-    far_send, vert_mine = lax.optimization_barrier((far_send, vert_mine))
+    far_send, vert_mine, halo_k, halo_v = lax.optimization_barrier(
+        (far_send, vert_mine, halo_k, halo_v)
+    )
     vert_other = lax.ppermute(vert_mine, AXES, [(i, i ^ 1) for i in range(devices)])
+    far_send, vert_other = lax.optimization_barrier((far_send, vert_other))
     far_got = lax.all_to_all(far_send, AXES, split_axis=0, concat_axis=0, tiled=True)
 
     my_far = lax.dynamic_slice_in_dim(far_blocks, rank * blocks, blocks, 1).reshape(-1)
@@ -210,7 +285,7 @@
     my_place = jnp.sum(same & (jnp.arange(reqs)[None, :] < jnp.arange(reqs)[:, None]), axis=1)
     got_slot = jnp.where(my_far >= 0, owner * CAP + jnp.minimum(my_place, CAP - 1), 0)
 
-    q_t = queries.reshape(tok, heads, group, dh).transpose(1, 2, 0, 3)
+    q_t = queries.reshape(tok, heads, group, dh).transpose(1, 0, 2, 3).reshape(heads, tok * group, dh)
     zero_at = jnp.argmax((slash_offsets == 0).astype(jnp.int32), axis=1)
     order = (zero_at[:, None] + jnp.arange(near)[None, :]) % near
     offsets = jnp.sum(
@@ -231,7 +306,7 @@
             num_scalar_prefetch=4,
             grid=(heads,),
             in_specs=[
-                by_head(group, tok, dh),
+                by_head(tok * group, dh),
                 by_head(tok, dh),
                 by_head(tok, dh),
                 by_head(halo_rows, dh),
@@ -240,7 +315,7 @@
                 pl.BlockSpec(memory_space=pl.ANY),
                 pl.BlockSpec(memory_space=pl.ANY),
             ],
-            out_specs=[by_head(blocks, rows, dh), by_head(blocks, 1, rows)],
+            out_specs=[by_head(blocks, rows, dh), by_head(blocks, rows)],
             scratch_shapes=[
                 pltpu.VMEM((halo_rows + tok, dh), jnp.bfloat16),
                 pltpu.VMEM((halo_rows + tok, dh), jnp.bfloat16),
@@ -251,9 +326,9 @@
         ),
         out_shape=[
             jax.ShapeDtypeStruct((heads, blocks, rows, dh), jnp.float32),
-            jax.ShapeDtypeStruct((heads, blocks, 1, rows), jnp.float32),
+            jax.ShapeDtypeStruct((heads, blocks, rows), jnp.float32),
         ],
-        compiler_params=pltpu.CompilerParams(vmem_limit_bytes=40 * 1024 * 1024),
+        compiler_params=pltpu.CompilerParams(vmem_limit_bytes=56 * 1024 * 1024),
         cost_estimate=pl.CostEstimate(
             flops=4 * heads * blocks * rows * dh * (near + verts) * BS,
             bytes_accessed=40_000_000,
@@ -265,37 +340,35 @@
         (vert_blocks // blocks).astype(jnp.int32),
         offsets.astype(jnp.int32),
         (rank * blocks).reshape(1).astype(jnp.int32),
-        q_t, k_t, v_t, before[0], before[1], vert_bias, vert_mine, vert_other,
-    )
-
-    attended = pl.pallas_call(
+        q_t, k_t, v_t, halo_k.transpose(1, 0, 2), halo_v.transpose(1, 0, 2), vert_bias, vert_mine, vert_other,
+    )
+
+    return pl.pallas_call(
         functools.partial(merge_kernel, heads=heads, blocks=blocks, group=group, scale=scale),
         grid_spec=pltpu.PrefetchScalarGridSpec(
             num_scalar_prefetch=2,
             grid=(blocks,),
             in_specs=[
-                pl.BlockSpec((heads, group, BS, dh), lambda b, *_: (0, 0, b, 0)),
+                pl.BlockSpec((heads, rows, dh), lambda b, *_: (0, b, 0)),
                 pl.BlockSpec((heads, 1, rows, dh), lambda b, *_: (0, b, 0, 0)),
-                pl.BlockSpec((heads, 1, 1, rows), lambda b, *_: (0, b, 0, 0)),
+                pl.BlockSpec((1, heads, rows), lambda b, *_: (b, 0, 0)),
                 pl.BlockSpec(memory_space=pl.ANY),
             ],
             out_specs=pl.BlockSpec((BS, q_heads, dh), lambda b, *_: (b, 0, 0)),
             scratch_shapes=[
                 pltpu.VMEM((2, heads, 2, BS, dh), jnp.bfloat16),
-                pltpu.VMEM((BS * q_heads, dh), jnp.float32),
                 pltpu.SemaphoreType.DMA((2,)),
             ],
         ),
         out_shape=jax.ShapeDtypeStruct((tok, q_heads, dh), jnp.bfloat16),
-        compiler_params=pltpu.CompilerParams(vmem_limit_bytes=40 * 1024 * 1024),
+        compiler_params=pltpu.CompilerParams(vmem_limit_bytes=56 * 1024 * 1024),
         cost_estimate=pl.CostEstimate(
             flops=4 * heads * blocks * rows * dh * BS,
             bytes_accessed=25_000_000,
             transcendentals=heads * blocks * rows * BS,
         ),
         name="far_merge",
-    )(got_slot.astype(jnp.int32), valid, q_t, local_out, local_lse, far_got)
-    return attended
+    )(got_slot.astype(jnp.int32), valid, q_t, local_out, local_lse.transpose(1, 0, 2), far_got)
 
 
 def solution(mesh):

time: 263 us -> 197 us (0.75)
  the two profiles are of different devices: /device:TPU:82 before, /device:TPU:90 now
where the time goes in v2:
time: 197 us; the launch traced here: 196 us
  Pallas kernels  79.3 us (40%)
  waiting for transfers between devices  61 us (31%)
  starting transfers between devices  24.6 us (12%)
  local copies, waits for them, and re-layouts  24.3 us (12%)
  other arithmetic  6.26 us (3%)
    pallas_call x1, Pallas kernels, shards(): pl.pallas_call(functools.partial(local_kernel, heads=heads, verts=verts,...  58 us
    all_to_all x1, waiting for transfers between devices, shards(): lax.all_to_all(far_send, AXES, split_axis=0, concat_axis=0, tiled=True)  31.1 us
    ppermute x1, waiting for transfers between devices, shards(): halo_v = lax.ppermute(values[tok - halo_rows:], AXES, forward)  17.9 us
    pallas_call x1, Pallas kernels, shards(): pl.pallas_call(functools.partial(merge_kernel, heads=heads, blocks=blocks...  16.6 us
    all_to_all x1, starting transfers between devices, shards(): lax.all_to_all(vert_send, AXES, split_axis=0, concat_axis=0, tiled=True)  10.3 us
    all_to_all x1, starting transfers between devices, shards(): lax.all_to_all(far_send, AXES, split_axis=0, concat_axis=0, tiled=True)  10.2 us
    gather x1, local copies, waits for them, and re-layouts, shards(): far_send = tiles[send_tile]  8.44 us
    ppermute x1, waiting for transfers between devices, shards(): halo_k = lax.ppermute(keys[tok - halo_rows:], AXES, forward)  7.59 us
  transfers between devices with their start and end apart: 5, of which 4 were waited for; matrix products, arithmetic and copies ran while one was open for 14% of the time, Pallas kernels for 32%

profile of v2, /device:TPU:90, one launch (start us, length us, event | category | flops | bytes accessed | tf_op | source)
XLA Modules:
  0.0 195.9 jit_solution(10360203740010282068)
XLA Ops:
  0.0 1.5 copy.45
  1.6 1.9 collective-permute-start
  3.5 0.6 reshape.232.vert_sm
  4.1 4.7 %vertical_pack.1 = bf16[128,64,128]{2,1,0:T(8,128)(2,1)} custom-call(s32[1]{0:T(128)} %bitcast.12.rank_sm, s32[96]{0:T(128)} %reshape.232.vert_sm, bf16[640,8,128]{2,1,0:T(8,128)(2,1)} %keys_hbm.1, bf16[640,8,128]{2,1,0:T(8,128)(2,1)} %values_hbm.1), custom_call_target="tpu_custom_call" | custom-call | tf_op jit(solution)/shard_map/vertical_pack/pallas_call | solution.py:239
  8.8 7.6 %collective-permute-done = bf16[448,8,128]{2,0,1:T(8,128)(2,1)} collective-permute-done((bf16[448,8,128]{2,0,1:T(8,128)(2,1)S(1)}, bf16[448,8,128]{2,0,1:T(8,128)(2,1)}, u32[]{:S(2)}, u32[]{:S(2)}) %collective-permute-start) | collective-permute-done | bytes 917536 | tf_op jit(solution)/shard_map/ppermute | solution.py:235
  16.4 10.3 %all-to-all-start = ((bf16[128,64,128]{2,1,0:T(8,128)(2,1)}), bf16[128,64,128]{2,1,0:T(8,128)(2,1)}, u32[]{:S(2)}, u32[]{:S(2)}) async-start(bf16[128,64,128]{2,1,0:T(8,128)(2,1)} %vertical_pack.1), calls=%async_computation | async-start | bytes 4194304 | tf_op jit(solution)/shard_map/all_to_all | solution.py:258
  27.0 2.1 %collective-permute-start.1 = (bf16[448,8,128]{2,0,1:T(8,128)(2,1)S(1)}, bf16[448,8,128]{2,0,1:T(8,128)(2,1)}, u32[]{:S(2)}, u32[]{:S(2)}) collective-permute-start(bf16[448,8,128]{2,0,1:T(8,128)(2,1)S(1)} %slice.11), channel_id=1, source_target_pairs={{0,1},{1,2},{2,3},{3,4},{4,5},{5,6},{6,7},{7,8},{8,9},{9,10},{10,1... | collective-permute-start | bytes 2752520 | tf_op jit(solution)/shard_map/ppermute | solution.py:236
  29.1 1.3 reshape.228
  31.3 2.0 pad_maximum_fusion
  33.2 8.4 %gather_fusion = bf16[256,2,64,128]{3,2,1,0:T(8,128)(2,1)} fusion(bf16[80,2,64,128]{3,2,0,1:T(8,128)(2,1)S(1)} %pad_maximum_fusion, s32[1024]{0:T(1024)S(1)} %pad_clamp_fusion), kind=kCustom, calls=%fused_computation | custom fusion | bytes 16778240 | tf_op jit(solution)/shard_map/gather | solution.py:273
  41.7 17.9 %collective-permute-done.1 = bf16[448,8,128]{2,0,1:T(8,128)(2,1)} collective-permute-done((bf16[448,8,128]{2,0,1:T(8,128)(2,1)S(1)}, bf16[448,8,128]{2,0,1:T(8,128)(2,1)}, u32[]{:S(2)}, u32[]{:S(2)}) %collective-permute-start.1) | collective-permute-done | bytes 917536 | tf_op jit(solution)/shard_map/ppermute | solution.py:236
  59.6 4.4 %collective-permute-done.2.other_hbm = bf16[128,64,128]{2,1,0:T(8,128)(2,1)S(1)} collective-permute-done((bf16[128,64,128]{2,1,0:T(8,128)(2,1)}, bf16[128,64,128]{2,1,0:T(8,128)(2,1)S(1)}, u32[]{:S(2)}, u32[]{:S(2)}) %collective-permute-start.2) | collective-permute-done | bytes 2097184 | tf_op jit(solution)/shard_map/ppermute | solution.py:277
  64.0 1.3 copy-done.5
  65.3 10.2 %all-to-all-start.1 = ((bf16[256,2,64,128]{3,2,1,0:T(8,128)(2,1)}), bf16[256,2,64,128]{3,2,1,0:T(8,128)(2,1)}, u32[]{:S(2)}, u32[]{:S(2)}) async-start(bf16[256,2,64,128]{3,2,1,0:T(8,128)(2,1)} %gather_fusion), calls=%async_computation.1 | async-start | bytes 16777216 | tf_op jit(solution)/shard_map/all_to_all | solution.py:279
  76.0 0.8 copy.37.bias_ref
  76.9 6.7 %copy.29 = bf16[640,8,4,128]{3,2,0,1:T(4,128)(2,1)} copy(bf16[640,8,4,128]{3,2,1,0:T(4,128)(2,1)} %bitcast.33) | data formatting | bytes 10485760 | tf_op jit(solution)/shard_map/reshape | solution.py:288
  84.1 0.7 copy.36.off_sm
  84.8 0.8 fusion.4
  85.8 0.8 dynamic-slice_divide_fusion
  87.9 0.6 add_select_fusion.1.slot_sm
  88.5 58.0 %local_attention.1 = (f32[8,10,256,128]{3,2,1,0:T(8,128)}, f32[8,10,256]{2,1,0:T(8,128)}) custom-call(s32[1]{0:T(128)} %bitcast.3.core_sm, s32[8,12]{1,0:T(8,128)} %add_select_fusion.1.slot_sm, s32[8,4]{1,0:T(8,128)} %copy.36.off_sm, s32[1]{0:T(128)} %bitcast.4.first_sm, bf16[8,2560,128]{2,1,0:T(8,128)(2,1)} %bitcast.27, bf16[8,640,128]{2,1,0:T(8,128)(2,1)} %bitcast.30, ...), custom_call_target="tpu_custom_call" | custom-call | flops 10737418240 | bytes 40000000 | tf_op jit(solution)/shard_map/local_attention/pallas_call | solution.py:300
  146.6 1.6 copy.44
  148.2 31.1 %all-to-all-done.1.far_hbm = bf16[256,2,64,128]{3,2,1,0:T(8,128)(2,1)} async-done(((bf16[256,2,64,128]{3,2,1,0:T(8,128)(2,1)}), bf16[256,2,64,128]{3,2,1,0:T(8,128)(2,1)}, u32[]{:S(2)}, u32[]{:S(2)}) %all-to-all-start.1) | async-done | bytes 8388640 | tf_op jit(solution)/shard_map/all_to_all | solution.py:279
  179.3 16.6 %far_merge.1 = bf16[640,32,128]{2,1,0:T(8,128)(2,1)} custom-call(s32[80]{0:T(128)} %add_select_fusion.4.slot_sm, s32[80]{0:T(128)} %convert_element_type.15.valid_sm, bf16[8,2560,128]{2,1,0:T(8,128)(2,1)} %bitcast.28, f32[8,10,256,128]{3,2,1,0:T(8,128)} %get-tuple-element.24.local_ref, f32[10,8,256]{2,1,0:T(8,128)} %bitcast.35, ...), custom_call_target="tpu_custom_call" | custom-call | flops 671088640 | bytes 25000000 | tf_op jit(solution)/shard_map/far_merge/pallas_call | solution.py:346
  (41 shorter events, 3.7 us)
Async XLA Ops:
  0.0 3.5 %copy-start.3 = (s32[8,12]{1,0:T(8,128)S(1)}, s32[8,12]{1,0:T(8,128)}, u32[]{:S(2)}) copy-start(s32[8,12]{1,0:T(8,128)} %param.9) | copy-start | bytes 1156
  1.5 7.3 %copy-start = (bf16[640,8,128]{2,0,1:T(8,128)(2,1)}, bf16[640,8,128]{2,0,1:T(8,128)(2,1)S(1)}, u32[]{:S(2)}) copy-start(bf16[640,8,128]{2,0,1:T(8,128)(2,1)S(1)} %copy.45) | copy-start | bytes 3932164
  1.6 14.8 %collective-permute-start = (bf16[448,8,128]{2,0,1:T(8,128)(2,1)S(1)}, bf16[448,8,128]{2,0,1:T(8,128)(2,1)}, u32[]{:S(2)}, u32[]{:S(2)}) collective-permute-start(bf16[448,8,128]{2,0,1:T(8,128)(2,1)S(1)} %slice.10), channel_id=1, source_target_pairs={{0,1},{1,2},{2,3},{3,4},{4,5},{5,6},{6,7},{7,8},{8,9},{9,10},{10,1... | collective-permute-start | bytes 2752520 | tf_op jit(solution)/shard_map/ppermute | solution.py:235
  8.8 18.0 %copy-start.2 = (bf16[640,8,128]{2,1,0:T(8,128)(2,1)S(1)}, bf16[640,8,128]{2,1,0:T(8,128)(2,1)}, u32[]{:S(2)}) copy-start(bf16[640,8,128]{2,1,0:T(8,128)(2,1)} %values_hbm.1) | copy-start | bytes 3932164
  16.4 43.2 %all-to-all-start = ((bf16[128,64,128]{2,1,0:T(8,128)(2,1)}), bf16[128,64,128]{2,1,0:T(8,128)(2,1)}, u32[]{:S(2)}, u32[]{:S(2)}) async-start(bf16[128,64,128]{2,1,0:T(8,128)(2,1)} %vertical_pack.1), calls=%async_computation | async-start | bytes 4194304 | tf_op jit(solution)/shard_map/all_to_all | solution.py:258
  26.9 4.3 %copy-start.1 = (bf16[640,8,128]{2,0,1:T(8,128)(2,1)}, bf16[640,8,128]{2,0,1:T(8,128)(2,1)S(1)}, u32[]{:S(2)}) copy-start(bf16[640,8,128]{2,0,1:T(8,128)(2,1)S(1)} %copy.46) | copy-start | bytes 3932164
  27.0 32.6 %collective-permute-start.1 = (bf16[448,8,128]{2,0,1:T(8,128)(2,1)S(1)}, bf16[448,8,128]{2,0,1:T(8,128)(2,1)}, u32[]{:S(2)}, u32[]{:S(2)}) collective-permute-start(bf16[448,8,128]{2,0,1:T(8,128)(2,1)S(1)} %slice.11), channel_id=1, source_target_pairs={{0,1},{1,2},{2,3},{3,4},{4,5},{5,6},{6,7},{7,8},{8,9},{9,10},{10,1... | collective-permute-start | bytes 2752520 | tf_op jit(solution)/shard_map/ppermute | solution.py:236
  59.6 4.4 %collective-permute-start.2 = (bf16[128,64,128]{2,1,0:T(8,128)(2,1)}, bf16[128,64,128]{2,1,0:T(8,128)(2,1)S(1)}, u32[]{:S(2)}, u32[]{:S(2)}) collective-permute-start(bf16[128,64,128]{2,1,0:T(8,128)(2,1)} %all-to-all-done.mine_hbm), channel_id=1, source_target_pairs={{0,1},{1,0},{2,3},{3,2},{4,5},{5,4},{6,7},{7,6},{8,9},{9,8},{10,11... | collective-permute-start | bytes 6291464 | tf_op jit(solution)/shard_map/ppermute | solution.py:277
  64.0 1.3 copy-start.5
  65.3 114.0 %all-to-all-start.1 = ((bf16[256,2,64,128]{3,2,1,0:T(8,128)(2,1)}), bf16[256,2,64,128]{3,2,1,0:T(8,128)(2,1)}, u32[]{:S(2)}, u32[]{:S(2)}) async-start(bf16[256,2,64,128]{3,2,1,0:T(8,128)(2,1)} %gather_fusion), calls=%async_computation.1 | async-start | bytes 16777216 | tf_op jit(solution)/shard_map/all_to_all | solution.py:279
  76.9 6.7 %copy-start.4 = (s32[8,4]{0,1:T(4,128)S(1)}, s32[8,4]{0,1:T(4,128)}, u32[]{:S(2)}) copy-start(s32[8,4]{0,1:T(4,128)} %param.10) | copy-start | bytes 388

commit v3 on v1

v3 whole, which is shorter than its diff:
```python
import functools

import jax
import jax.numpy as jnp
from jax import lax
from jax.experimental import pallas as pl
from jax.experimental.pallas import tpu as pltpu
from jax.sharding import PartitionSpec as P

BS = 64
NW = 8
CAP = 2
AXES = ("blk", "grid")
MASKED = -1e30
LOG2E = 1.4426950408889634


def local_kernel(
    core_sm, slot_sm, off_sm, first_sm,
    q_ref, ko_ref, vo_ref, kh_ref, vh_ref, bias_ref, mine_hbm, other_hbm,
    out_ref, lse_ref,
    kx, vx, kv_buf, vv_buf, lse_buf, sems,
    *, heads, verts, blocks, group, near, scale,
):
    h = pl.program_id(0)
    halo = kh_ref.shape[1]
    own = ko_ref.shape[1]
    dh = q_ref.shape[2]
    left = pl.ds(0, dh)

    def fetch(head, buf):
        def copies(k_from, v_from):
            for i in range(verts):
                slot = slot_sm[head, i]
                rows = pl.ds(i * BS, BS)
                pltpu.make_async_copy(
                    k_from(slot), kv_buf.at[buf, rows], sems.at[buf, 0]
                ).start()
                pltpu.make_async_copy(
                    v_from(slot), vv_buf.at[buf, rows, left], sems.at[buf, 1]
                ).start()

        mine = lambda slot: mine_hbm.at[slot, 2]
        other = lambda slot: other_hbm.at[slot]

        @pl.when(core_sm[0] == 0)
        def _():
            copies(mine, other)

        @pl.when(core_sm[0] != 0)
        def _():
            copies(other, mine)

    @pl.when(h == 0)
    def _():
        vx[:, dh:] = jnp.ones((halo + own, dh), jnp.bfloat16)
        for buf in range(2):
            vv_buf[buf, :, dh:] = jnp.ones((verts * BS, dh), jnp.bfloat16)
        fetch(0, 0)

    @pl.when(h + 1 < heads)
    def _():
        fetch(h + 1, (h + 1) % 2)

    kx[0:halo] = kh_ref[0]
    kx[halo : halo + own] = ko_ref[0]
    vx[0:halo, :dh] = vh_ref[0]
    vx[halo : halo + own, :dh] = vo_ref[0]
    cur = h % 2
    pltpu.make_async_copy(kv_buf.at[cur], kv_buf.at[cur], sems.at[cur, 0]).wait()
    pltpu.make_async_copy(
        vv_buf.at[cur, :, left], vv_buf.at[cur, :, left], sems.at[cur, 1]
    ).wait()

    t_pos = lax.broadcasted_iota(jnp.int32, (group * BS, near * BS), 0) // group
    u_pos = lax.broadcasted_iota(jnp.int32, (group * BS, near * BS), 1)
    causal_bias = jnp.where((u_pos < BS) & (u_pos > t_pos), MASKED, 0.0)
    lane = lax.broadcasted_iota(jnp.int32, (1, near * BS), 1) // BS

    def one_block(b, carry):
        rows = pl.multiple_of(b * group * BS, group * BS)
        q = q_ref[0, pl.ds(rows, group * BS), :]
        k_parts = []
        v_parts = []
        row_bias = jnp.zeros((1, near * BS), jnp.float32)
        for i in range(near):
            off = off_sm[h, i]
            start = pl.multiple_of((b + NW - 1 - off) * BS, BS)
            k_parts.append(kx[pl.ds(start, BS), :])
            v_parts.append(vx[pl.ds(start, BS), :])
            miss = jnp.where(first_sm[0] + b < off, MASKED, 0.0)
            row_bias = jnp.where(lane == i, miss, row_bias)
        k_near = jnp.concatenate(k_parts, axis=0)
        v_near = jnp.concatenate(v_parts, axis=0)
        dims = (((1,), (1,)), ((), ()))
        s_near = lax.dot_general(q, k_near, dims, preferred_element_type=jnp.float32)
        s_near = s_near + (causal_bias + row_bias)
        s_vert = lax.dot_general(q, kv_buf[cur], dims, preferred_element_type=jnp.float32)
        s_vert = s_vert + bias_ref[0, pl.ds(b, 1), :]
        top = jnp.maximum(
            jnp.max(s_near, axis=1, keepdims=True), jnp.max(s_vert, axis=1, keepdims=True)
        )
        p_near = jnp.exp2((s_near - top) * (scale * LOG2E)).astype(jnp.bfloat16)
        p_vert = jnp.exp2((s_vert - top) * (scale * LOG2E)).astype(jnp.bfloat16)
        acc = jnp.dot(p_near, v_near, preferred_element_type=jnp.float32)
        acc = acc + jnp.dot(p_vert, vv_buf[cur], preferred_element_type=jnp.float32)
        total = acc[:, dh:]
        out_ref[0, b] = acc[:, :dh] / total
        column = lax.broadcasted_iota(jnp.int32, total.shape, 1) == b
        lse_buf[...] = jnp.where(column, top * scale + jnp.log(total), lse_buf[...])
        return carry

    lax.fori_loop(0, blocks, one_block, 0, unroll=True)
    lse_ref[0] = lse_buf[...].T[:blocks]


def pack_kernel(tile_sm, vert_sm, k_ref, v_ref, out_ref):
    base = pl.program_id(0) * out_ref.shape[0]
    for d in range(out_ref.shape[0]):
        tile = tile_sm[base + d]
        out_ref[d, 0] = k_ref[tile]
        out_ref[d, 1] = v_ref[tile]
        out_ref[d, 2] = (v_ref if d % 2 else k_ref)[vert_sm[0]]


def merge_kernel(
    owner_sm, place_sm, valid_sm,
    q_ref, local_ref, lse_ref, first_hbm, second_hbm,
    out_ref,
    kv_buf, sems,
    *, heads, blocks, group, per, scale,
):
    step = pl.program_id(0)

    def fetch(at, buf):
        for j in range(per):
            for h in range(heads):
                request = h * blocks + at * per + j
                owner = owner_sm[request]
                to = kv_buf.at[buf, j, h]

                @pl.when(place_sm[request] == 0)
                def _():
                    pltpu.make_async_copy(
                        first_hbm.at[owner, pl.ds(0, 2)], to, sems.at[buf]
                    ).start()

                @pl.when(place_sm[request] != 0)
                def _():
                    pltpu.make_async_copy(second_hbm.at[owner], to, sems.at[buf]).start()

    @pl.when(step == 0)
    def _():
        fetch(0, 0)

    @pl.when(step + 1 < blocks // per)
    def _():
        fetch(step + 1, (step + 1) % 2)

    cur = step % 2
    pltpu.make_async_copy(kv_buf.at[cur], kv_buf.at[cur], sems.at[cur]).wait()
    rows = group * BS
    dh = q_ref.shape[2]
    head_row = lax.broadcasted_iota(jnp.int32, (heads, 1), 0)
    low = lax.broadcasted_iota(jnp.int32, (rows // 8, 8, dh), 1) < group
    for j in range(per):
        weights = []
        tops = []
        totals = []
        for h in range(heads):
            s = lax.dot_general(
                kv_buf[cur, j, h, 0], q_ref[h, j * rows : (j + 1) * rows, :],
                (((1,), (1,)), ((), ())), preferred_element_type=jnp.float32,
            )
            top = jnp.max(s, axis=0, keepdims=True)
            p = jnp.exp2((s - top) * (scale * LOG2E))
            weights.append(p)
            tops.append(top)
            totals.append(jnp.sum(p, axis=0, keepdims=True))
        total = jnp.concatenate(totals, axis=0)
        far_lse = jnp.concatenate(tops, axis=0) * scale + jnp.log(total)
        local_lse = lse_ref[j]
        joint = jnp.maximum(local_lse, far_lse)
        valid = jnp.zeros((heads, 1), jnp.int32)
        for h in range(heads):
            valid = jnp.where(head_row == h, valid_sm[h * blocks + step * per + j], valid)
        a = jnp.where(valid > 0, jnp.exp(local_lse - joint), 1.0)
        c = jnp.where(valid > 0, jnp.exp(far_lse - joint), 0.0)
        local_share = (a / (a + c)).T
        far_share = c / ((a + c) * total)

        for quad in range(heads // 4):
            wide = []
            for pair in (2 * quad, 2 * quad + 1):
                halves = []
                for h in (2 * pair, 2 * pair + 1):
                    p = (weights[h] * far_share[h : h + 1]).astype(jnp.bfloat16)
                    acc = lax.dot_general(
                        p, kv_buf[cur, j, h, 1], (((0,), (0,)), ((), ())),
                        preferred_element_type=jnp.float32,
                    )
                    mixed = local_share[:, h : h + 1] * local_ref[h, j] + acc
                    halves.append(mixed.reshape(rows // 8, 8, dh))
                x, y = halves
                even = jnp.where(low, x, pltpu.roll(y, group, 1))
                odd = jnp.where(low, pltpu.roll(x, group, 1), y)
                wide.append(jnp.stack([even, odd], axis=1).reshape(BS, 8, dh))
            both = jnp.concatenate(wide, axis=1)
            out_ref[j * BS : (j + 1) * BS, quad * 16 : (quad + 1) * 16, :] = both.astype(
                jnp.bfloat16
            )


def shards(queries, keys, values, vert_blocks, slash_offsets, far_blocks):
    tok, q_heads, dh = queries.shape
    heads = keys.shape[1]
    group = q_heads // heads
    blocks = tok // BS
    verts = vert_blocks.shape[1]
    near = slash_offsets.shape[1]
    reqs = heads * blocks
    devices = lax.axis_size(AXES)
    rank = lax.axis_index(AXES)
    core = rank % 2
    scale = dh**-0.5
    halo_rows = (NW - 1) * BS
    rows = group * BS

    forward = [(i, i + 1) for i in range(devices - 1)]
    halo_k = lax.ppermute(keys[tok - halo_rows :], AXES, forward)
    halo_v = lax.ppermute(values[tok - halo_rows :], AXES, forward)

    k_t = keys.transpose(1, 0, 2)
    v_t = values.transpose(1, 0, 2)
    tiles = jnp.concatenate(
        [k_t.reshape(reqs, BS, dh), v_t.reshape(reqs, BS, dh)], axis=0
    )

    vert_here = vert_blocks - rank * blocks
    vert_tile = jnp.max(
        jnp.where(
            (vert_here >= 0) & (vert_here < blocks),
            vert_here + jnp.arange(heads)[:, None] * blocks,
            0,
        )
    )

    all_far = far_blocks.reshape(heads, devices, blocks).transpose(1, 0, 2).reshape(devices, reqs)
    earlier = (jnp.arange(reqs)[:, None] < jnp.arange(reqs)[None, :]).astype(jnp.float32)
    asked = (all_far >= 0) & (all_far // blocks == rank)
    place = jnp.dot(asked.astype(jnp.float32), earlier).astype(jnp.int32)
    tile = (jnp.arange(reqs)[None, :] // blocks) * blocks + all_far - rank * blocks
    wanted = asked[:, None, :] & (place[:, None, :] == jnp.arange(CAP)[None, :, None])
    send_tile = jnp.max(jnp.where(wanted, tile[:, None, :], 0), axis=2)
    second = send_tile[:, 1:]
    chunk = 16
    whole = pl.BlockSpec((reqs, BS, dh), lambda i, *_: (0, 0, 0))
    first_send = pl.pallas_call(
        pack_kernel,
        grid_spec=pltpu.PrefetchScalarGridSpec(
            num_scalar_prefetch=2,
            grid=(devices // chunk,),
            in_specs=[whole, whole],
            out_specs=pl.BlockSpec((chunk, 3, BS, dh), lambda i, *_: (i, 0, 0, 0)),
        ),
        out_shape=jax.ShapeDtypeStruct((devices, 3, BS, dh), jnp.bfloat16),
        compiler_params=pltpu.CompilerParams(vmem_limit_bytes=32 * 1024 * 1024),
        name="pack_first",
    )(
        send_tile[:, 0], vert_tile.reshape(1),
        k_t.reshape(reqs, BS, dh), v_t.reshape(reqs, BS, dh),
    )
    first_send, halo_k = lax.optimization_barrier((first_send, halo_k))
    first_got = lax.all_to_all(first_send, AXES, split_axis=0, concat_axis=0, tiled=True)
    second_send = tiles[jnp.concatenate([second, second + reqs], axis=1)]
    my_far = lax.dynamic_slice_in_dim(far_blocks, rank * blocks, blocks, 1).reshape(-1)
    valid = (my_far >= 0).astype(jnp.int32)
    owner = jnp.where(my_far >= 0, my_far // blocks, -1)
    same = owner[:, None] == owner[None, :]
    my_place = jnp.sum(same & (jnp.arange(reqs)[None, :] < jnp.arange(reqs)[:, None]), axis=1)

    q_t = queries.reshape(tok, heads, group, dh).transpose(1, 0, 2, 3).reshape(heads, tok * group, dh)
    zero_at = jnp.argmax((slash_offsets == 0).astype(jnp.int32), axis=1)
    order = (zero_at[:, None] + jnp.arange(near)[None, :]) % near
    offsets = jnp.sum(
        jnp.where(order[:, :, None] == jnp.arange(near)[None, None, :], slash_offsets[:, None, :], 0),
        axis=2,
    )
    my_blocks = rank * blocks + jnp.arange(blocks)
    vert_ok = vert_blocks[:, None, :] <= my_blocks[None, :, None] - NW
    vert_bias = jnp.repeat(jnp.where(vert_ok, 0.0, MASKED).astype(jnp.float32), BS, axis=2)

    owner_at = jnp.maximum(owner, 0).astype(jnp.int32)
    my_place = my_place.astype(jnp.int32)
    offsets = offsets.astype(jnp.int32)
    second_send, first_got, halo_k, halo_v, q_t, vert_bias, offsets, owner_at, my_place, valid = (
        lax.optimization_barrier(
            (
                second_send, first_got, halo_k, halo_v,
                q_t, vert_bias, offsets, owner_at, my_place, valid,
            )
        )
    )
    vert_other = lax.ppermute(first_got[:, 2], AXES, [(i, i ^ 1) for i in range(devices)])
    second_send, vert_other = lax.optimization_barrier((second_send, vert_other))
    second_got = lax.all_to_all(second_send, AXES, split_axis=0, concat_axis=0, tiled=True)

    by_head = lambda *tail: pl.BlockSpec((1,) + tail, lambda h, *_: (h,) + (0,) * len(tail))
    local_out, local_lse = pl.pallas_call(
        functools.partial(
            local_kernel, heads=heads, verts=verts, blocks=blocks, group=group, near=near,
            scale=scale,
        ),
        grid_spec=pltpu.PrefetchScalarGridSpec(
            num_scalar_prefetch=4,
            grid=(heads,),
            in_specs=[
                by_head(tok * group, dh),
                by_head(tok, dh),
                by_head(tok, dh),
                by_head(halo_rows, dh),
                by_head(halo_rows, dh),
                by_head(blocks, verts * BS),
                pl.BlockSpec(memory_space=pltpu.HBM),
                pl.BlockSpec(memory_space=pltpu.HBM),
            ],
            out_specs=[by_head(blocks, rows, dh), by_head(blocks, rows)],
            scratch_shapes=[
                pltpu.VMEM((halo_rows + tok, dh), jnp.bfloat16),
                pltpu.VMEM((halo_rows + tok, 2 * dh), jnp.bfloat16),
                pltpu.VMEM((2, verts * BS, dh), jnp.bfloat16),
                pltpu.VMEM((2, verts * BS, 2 * dh), jnp.bfloat16),
                pltpu.VMEM((rows, 128), jnp.float32),
                pltpu.SemaphoreType.DMA((2, 2)),
            ],
        ),
        out_shape=[
            jax.ShapeDtypeStruct((heads, blocks, rows, dh), jnp.float32),
            jax.ShapeDtypeStruct((heads, blocks, rows), jnp.float32),
        ],
        compiler_params=pltpu.CompilerParams(vmem_limit_bytes=56 * 1024 * 1024),
        cost_estimate=pl.CostEstimate(
            flops=4 * heads * blocks * rows * dh * (near + verts) * BS,
            bytes_accessed=40_000_000,
            transcendentals=heads * blocks * rows * (near + verts) * BS,
        ),
        name="local_attention",
    )(
        core.reshape(1).astype(jnp.int32),
        (vert_blocks // blocks).astype(jnp.int32),
        offsets,
        (rank * blocks).reshape(1).astype(jnp.int32),
        q_t, k_t, v_t, halo_k.transpose(1, 0, 2), halo_v.transpose(1, 0, 2), vert_bias, first_got, vert_other,
    )

    per = 2 if blocks % 2 == 0 else 1
    return pl.pallas_call(
        functools.partial(
            merge_kernel, heads=heads, blocks=blocks, group=group, per=per, scale=scale
        ),
        grid_spec=pltpu.PrefetchScalarGridSpec(
            num_scalar_prefetch=3,
            grid=(blocks // per,),
            in_specs=[
                pl.BlockSpec((heads, per * rows, dh), lambda b, *_: (0, b, 0)),
                pl.BlockSpec((heads, per, rows, dh), lambda b, *_: (0, b, 0, 0)),
                pl.BlockSpec((per, heads, rows), lambda b, *_: (b, 0, 0)),
                pl.BlockSpec(memory_space=pl.ANY),
                pl.BlockSpec(memory_space=pl.ANY),
            ],
            out_specs=pl.BlockSpec((per * BS, q_heads, dh), lambda b, *_: (b, 0, 0)),
            scratch_shapes=[
                pltpu.VMEM((2, per, heads, 2, BS, dh), jnp.bfloat16),
                pltpu.SemaphoreType.DMA((2,)),
            ],
        ),
        out_shape=jax.ShapeDtypeStruct((tok, q_heads, dh), jnp.bfloat16),
        compiler_params=pltpu.CompilerParams(vmem_limit_bytes=56 * 1024 * 1024),
        cost_estimate=pl.CostEstimate(
            flops=4 * heads * blocks * rows * dh * BS,
            bytes_accessed=25_000_000,
            transcendentals=heads * blocks * rows * BS,
        ),
        name="far_merge",
    )(
        owner_at, my_place, valid,
        q_t, local_out, local_lse.transpose(1, 0, 2), first_got, second_got,
    )


def solution(mesh):
    split = P(AXES, None, None)
    return jax.shard_map(
        shards,
        mesh=mesh,
        in_specs=(split, split, split, P(), P(), P()),
        out_specs=split,
        check_vma=False,
    )
```

time: 263 us -> 194 us (0.74)
  the two profiles are of different devices: /device:TPU:82 before, /device:TPU:1 now
where the time goes in v3:
time: 194 us; the launch traced here: 193 us
  waiting for transfers between devices  76.3 us (39%)
  Pallas kernels  52.3 us (27%)
  starting transfers between devices  30.7 us (16%)
  local copies, waits for them, and re-layouts  24.4 us (13%)
  other arithmetic  8 us (4%)
    ppermute x1, waiting for transfers between devices, shards(): halo_v = lax.ppermute(values[tok - halo_rows:], AXES, forward)  56.3 us
    pallas_call x1, Pallas kernels, shards(): pl.pallas_call(functools.partial(local_kernel, heads=heads, verts=verts,...  34.3 us
    pallas_call x1, Pallas kernels, shards(): pl.pallas_call(functools.partial(merge_kernel, heads=heads, blocks=blocks...  16.3 us
    all_to_all x1, waiting for transfers between devices, shards(): lax.all_to_all(second_send, AXES, split_axis=0, concat_axis=0, tiled=True)  15.2 us
    all_to_all x1, starting transfers between devices, shards(): lax.all_to_all(first_send, AXES, split_axis=0, concat_axis=0, tiled=True)  11.9 us
    all_to_all x1, starting transfers between devices, shards(): lax.all_to_all(second_send, AXES, split_axis=0, concat_axis=0, tiled=True)  10.7 us
    unnamed x26, local copies, waits for them, and re-layouts  7.01 us
    reshape x1, local copies, waits for them, and re-layouts, shards(): queries.reshape(tok, heads, group, dh).transpose(1, 0, 2, 3)  6.74 us
  transfers between devices with their start and end apart: 5, of which 4 were waited for; matrix products, arithmetic and copies ran while one was open for 13% of the time, Pallas kernels for 19%

profile of v3, /device:TPU:1, one launch (start us, length us, event | category | flops | bytes accessed | tf_op | source)
XLA Modules:
  0.0 193.0 jit_solution(10267855490933298422)
XLA Ops:
  0.0 1.5 copy.47
  1.6 4.5 %collective-permute-start = (bf16[448,8,128]{2,0,1:T(8,128)(2,1)S(1)}, bf16[448,8,128]{2,0,1:T(8,128)(2,1)}, u32[]{:S(2)}, u32[]{:S(2)}) collective-permute-start(bf16[448,8,128]{2,0,1:T(8,128)(2,1)S(1)} %slice.22), channel_id=1, source_target_pairs={{0,1},{1,2},{2,3},{3,4},{4,5},{5,6},{6,7},{7,8},{8,9},{9,10},{10,1... | collective-permute-start | bytes 2752520 | tf_op jit(solution)/shard_map/ppermute | solution.py:230
  6.9 0.8 convolution_convert_fusion
  8.2 1.5 copy.46
  9.9 1.4 add_select_fusion.1
  11.4 1.7 pack_first.1
  13.1 2.6 %copy-done = bf16[128,3,64,128]{3,2,1,0:T(8,128)(2,1)} copy-done((bf16[128,3,64,128]{3,2,1,0:T(8,128)(2,1)}, bf16[128,3,64,128]{3,2,1,0:T(8,128)(2,1)S(1)}, u32[]{:S(2)}) %copy-start) | copy-done | bytes 6291480
  16.4 11.9 %all-to-all-start = ((bf16[128,3,64,128]{3,2,1,0:T(8,128)(2,1)}), bf16[128,3,64,128]{3,2,1,0:T(8,128)(2,1)}, u32[]{:S(2)}, u32[]{:S(2)}) async-start(bf16[128,3,64,128]{3,2,1,0:T(8,128)(2,1)} %copy-done), calls=%async_computation | async-start | bytes 12582912 | tf_op jit(solution)/shard_map/all_to_all | solution.py:274
  28.3 1.0 slice.23
  29.3 3.5 %collective-permute-start.1 = (bf16[448,8,128]{2,0,1:T(8,128)(2,1)}, bf16[448,8,128]{2,0,1:T(8,128)(2,1)}, u32[]{:S(2)}, u32[]{:S(2)}) collective-permute-start(bf16[448,8,128]{2,0,1:T(8,128)(2,1)} %slice.23), channel_id=1, source_target_pairs={{0,1},{1,2},{2,3},{3,4},{4,5},{5,6},{6,7},{7,8},{8,9},{9,10},{10,1... | collective-permute-start | bytes 2752520 | tf_op jit(solution)/shard_map/ppermute | solution.py:231
  33.9 1.7 pad_maximum_fusion
  35.7 0.8 fusion.4
  37.8 6.7 %copy.36 = bf16[640,8,4,128]{3,2,0,1:T(4,128)(2,1)} copy(bf16[640,8,4,128]{3,2,1,0:T(4,128)(2,1)} %bitcast.48) | data formatting | bytes 10485760 | tf_op jit(solution)/shard_map/reshape | solution.py:282
  44.5 3.1 %gather_fusion = bf16[256,64,128]{2,1,0:T(8,128)(2,1)} fusion(bf16[160,64,128]{2,1,0:T(8,128)(2,1)S(1)} %copy-done.3, s32[1024]{0:T(1024)S(1)} %pad_clamp_fusion), kind=kCustom, calls=%fused_computation | custom fusion | bytes 8389632 | tf_op jit(solution)/shard_map/gather | solution.py:275
  49.5 56.3 %collective-permute-done.1 = bf16[448,8,128]{2,0,1:T(8,128)(2,1)} collective-permute-done((bf16[448,8,128]{2,0,1:T(8,128)(2,1)}, bf16[448,8,128]{2,0,1:T(8,128)(2,1)}, u32[]{:S(2)}, u32[]{:S(2)}) %collective-permute-start.1) | collective-permute-done | bytes 917536 | tf_op jit(solution)/shard_map/ppermute | solution.py:231
  105.9 1.8 slice_bitcast_fusion
  107.8 4.1 %collective-permute-done.2.other_hbm = bf16[128,64,128]{2,1,0:T(8,128)(2,1)S(1)} collective-permute-done((bf16[128,64,128]{2,1,0:T(8,128)(2,1)S(1)}, bf16[128,64,128]{2,1,0:T(8,128)(2,1)S(1)}, u32[]{:S(2)}, u32[]{:S(2)}) %collective-permute-start.2) | collective-permute-done | bytes 2097184 | tf_op jit(solution)/shard_map/ppermute | solution.py:304
  111.9 1.3 copy-done.11
  113.2 10.7 %all-to-all-start.1 = ((bf16[128,2,64,128]{3,2,1,0:T(8,128)(2,1)}), bf16[128,2,64,128]{3,2,1,0:T(8,128)(2,1)}, u32[]{:S(2)}, u32[]{:S(2)}) async-start(bf16[128,2,64,128]{3,2,1,0:T(8,128)(2,1)} %bitcast.47), calls=%async_computation.1 | async-start | bytes 8388608 | tf_op jit(solution)/shard_map/all_to_all | solution.py:306
  124.6 0.8 copy.38.bias_ref
  125.4 34.3 %local_attention.1 = (f32[8,10,256,128]{3,2,1,0:T(8,128)}, f32[8,10,256]{2,1,0:T(8,128)}) custom-call(s32[1]{0:T(128)} %bitcast.15.core_sm, s32[8,12]{1,0:T(8,128)} %get-tuple-element.47.slot_sm, s32[8,4]{1,0:T(8,128)} %copy.37.off_sm, s32[1]{0:T(128)} %bitcast.16.first_sm, bf16[8,2560,128]{2,1,0:T(8,128)(2,1)} %bitcast.45, bf16[8,640,128]{2,1,0:T(8,128)(2,1)} %bitcast.41, ...), custom_call_target="tpu_custom_call" | custom-call | flops 10737418240 | bytes 40000000 | tf_op jit(solution)/shard_map/local_attention/pallas_call | solution.py:309
  159.7 1.6 copy.45
  161.3 15.2 %all-to-all-done.1.second_hbm = bf16[128,2,64,128]{3,2,1,0:T(8,128)(2,1)} async-done(((bf16[128,2,64,128]{3,2,1,0:T(8,128)(2,1)}), bf16[128,2,64,128]{3,2,1,0:T(8,128)(2,1)}, u32[]{:S(2)}, u32[]{:S(2)}) %all-to-all-start.1) | async-done | bytes 4194336 | tf_op jit(solution)/shard_map/all_to_all | solution.py:306
  176.5 16.3 %far_merge.1 = bf16[640,32,128]{2,1,0:T(8,128)(2,1)} custom-call(s32[80]{0:T(128)} %get-tuple-element.25.owner_sm, s32[80]{0:T(128)} %convert_reduce_fusion.place_sm, s32[80]{0:T(128)} %convert_element_type.17.valid_sm, bf16[8,2560,128]{2,1,0:T(8,128)(2,1)} %bitcast.46, f32[8,10,256,128]{3,2,1,0:T(8,128)} %get-tuple-element.36.local_ref, ...), custom_call_target="tpu_custom_call" | custom-call | flops 671088640 | bytes 25000000 | tf_op jit(solution)/shard_map/far_merge/pallas_call | solution.py:357
  (54 shorter events, 7.2 us)
Async XLA Ops:
  0.0 6.1 %copy-start.6 = (s32[8,1280]{1,0:T(8,128)S(1)}, s32[8,1280]{1,0:T(8,128)}, u32[]{:S(2)}) copy-start(s32[8,1280]{1,0:T(8,128)} %param.11) | copy-start | bytes 122884
  1.5 32.4 %copy-start.1 = (bf16[640,8,128]{2,0,1:T(8,128)(2,1)}, bf16[640,8,128]{2,0,1:T(8,128)(2,1)S(1)}, u32[]{:S(2)}) copy-start(bf16[640,8,128]{2,0,1:T(8,128)(2,1)S(1)} %copy.47) | copy-start | bytes 3932164
  1.5 8.4 %copy-start.8 = (s32[8,12]{1,0:T(8,128)S(1)}, s32[8,12]{1,0:T(8,128)}, u32[]{:S(2)}) copy-start(s32[8,12]{1,0:T(8,128)} %param.9) | copy-start | bytes 1156
  1.6 14.8 %collective-permute-start = (bf16[448,8,128]{2,0,1:T(8,128)(2,1)S(1)}, bf16[448,8,128]{2,0,1:T(8,128)(2,1)}, u32[]{:S(2)}, u32[]{:S(2)}) collective-permute-start(bf16[448,8,128]{2,0,1:T(8,128)(2,1)S(1)} %slice.22), channel_id=1, source_target_pairs={{0,1},{1,2},{2,3},{3,4},{4,5},{5,6},{6,7},{7,8},{8,9},{9,10},{10,1... | collective-permute-start | bytes 2752520 | tf_op jit(solution)/shard_map/ppermute | solution.py:230
  6.8 1.4 copy-start.4
  8.2 1.5 copy-start.5
  8.2 1.6 copy-start.7
  8.2 1.7 copy-start.10
  9.8 24.2 %copy-start.2 = (bf16[640,8,128]{2,0,1:T(8,128)(2,1)}, bf16[640,8,128]{2,0,1:T(8,128)(2,1)S(1)}, u32[]{:S(2)}) copy-start(bf16[640,8,128]{2,0,1:T(8,128)(2,1)S(1)} %copy.46) | copy-start | bytes 3932164
  13.1 2.7 %copy-start = (bf16[128,3,64,128]{3,2,1,0:T(8,128)(2,1)}, bf16[128,3,64,128]{3,2,1,0:T(8,128)(2,1)S(1)}, u32[]{:S(2)}) copy-start(bf16[128,3,64,128]{3,2,1,0:T(8,128)(2,1)S(1)} %pack_first.1) | copy-start | bytes 18874372
  16.4 89.5 %all-to-all-start = ((bf16[128,3,64,128]{3,2,1,0:T(8,128)(2,1)}), bf16[128,3,64,128]{3,2,1,0:T(8,128)(2,1)}, u32[]{:S(2)}, u32[]{:S(2)}) async-start(bf16[128,3,64,128]{3,2,1,0:T(8,128)(2,1)} %copy-done), calls=%async_computation | async-start | bytes 12582912 | tf_op jit(solution)/shard_map/all_to_all | solution.py:274
  29.3 76.6 %collective-permute-start.1 = (bf16[448,8,128]{2,0,1:T(8,128)(2,1)}, bf16[448,8,128]{2,0,1:T(8,128)(2,1)}, u32[]{:S(2)}, u32[]{:S(2)}) collective-permute-start(bf16[448,8,128]{2,0,1:T(8,128)(2,1)} %slice.23), channel_id=1, source_target_pairs={{0,1},{1,2},{2,3},{3,4},{4,5},{5,6},{6,7},{7,8},{8,9},{9,10},{10,1... | collective-permute-start | bytes 2752520 | tf_op jit(solution)/shard_map/ppermute | solution.py:231
  37.8 6.8 %copy-start.3 = (bf16[160,64,128]{2,1,0:T(8,128)(2,1)S(1)}, bf16[160,64,128]{2,1,0:T(8,128)(2,1)}, u32[]{:S(2)}) copy-start(bf16[160,64,128]{2,1,0:T(8,128)(2,1)} %pad_maximum_fusion) | copy-start | bytes 7864324
  44.5 3.1 %copy-start.9 = (s32[8,4]{0,1:T(4,128)S(1)}, s32[8,4]{0,1:T(4,128)}, u32[]{:S(2)}) copy-start(s32[8,4]{0,1:T(4,128)} %param.10) | copy-start | bytes 388
  107.7 4.2 %collective-permute-start.2 = (bf16[128,64,128]{2,1,0:T(8,128)(2,1)S(1)}, bf16[128,64,128]{2,1,0:T(8,128)(2,1)S(1)}, u32[]{:S(2)}, u32[]{:S(2)}) collective-permute-start(bf16[128,64,128]{2,1,0:T(8,128)(2,1)S(1)} %slice_bitcast_fusion), channel_id=1, source_target_pairs={{0,1},{1,0},{2,3},{3,2},{4,5},{5,4},{6,7},{7,6},{8,9},{9,8},{10,11... | collective-permute-start | bytes 6291464 | tf_op jit(solution)/shard_map/ppermute | solution.py:304
  111.9 1.3 copy-start.11
  113.2 63.3 %all-to-all-start.1 = ((bf16[128,2,64,128]{3,2,1,0:T(8,128)(2,1)}), bf16[128,2,64,128]{3,2,1,0:T(8,128)(2,1)}, u32[]{:S(2)}, u32[]{:S(2)}) async-start(bf16[128,2,64,128]{3,2,1,0:T(8,128)(2,1)} %bitcast.47), calls=%async_computation.1 | async-start | bytes 8388608 | tf_op jit(solution)/shard_map/all_to_all | solution.py:306

commit v4 on v3

--- a/solution.py
+++ b/solution.py
@@ -123,6 +123,14 @@
         out_ref[d, 2] = (v_ref if d % 2 else k_ref)[vert_sm[0]]
 
 
+def pack_second_kernel(tile_sm, k_ref, v_ref, out_ref):
+    base = pl.program_id(0) * out_ref.shape[0]
+    for d in range(out_ref.shape[0]):
+        tile = tile_sm[base + d]
+        out_ref[d, 0] = k_ref[tile]
+        out_ref[d, 1] = v_ref[tile]
+
+
 def merge_kernel(
     owner_sm, place_sm, valid_sm,
     q_ref, local_ref, lse_ref, first_hbm, second_hbm,
@@ -232,9 +240,6 @@
 
     k_t = keys.transpose(1, 0, 2)
     v_t = values.transpose(1, 0, 2)
-    tiles = jnp.concatenate(
-        [k_t.reshape(reqs, BS, dh), v_t.reshape(reqs, BS, dh)], axis=0
-    )
 
     vert_here = vert_blocks - rank * blocks
     vert_tile = jnp.max(
@@ -252,7 +257,6 @@
     tile = (jnp.arange(reqs)[None, :] // blocks) * blocks + all_far - rank * blocks
     wanted = asked[:, None, :] & (place[:, None, :] == jnp.arange(CAP)[None, :, None])
     send_tile = jnp.max(jnp.where(wanted, tile[:, None, :], 0), axis=2)
-    second = send_tile[:, 1:]
     chunk = 16
     whole = pl.BlockSpec((reqs, BS, dh), lambda i, *_: (0, 0, 0))
     first_send = pl.pallas_call(
@@ -270,9 +274,23 @@
         send_tile[:, 0], vert_tile.reshape(1),
         k_t.reshape(reqs, BS, dh), v_t.reshape(reqs, BS, dh),
     )
-    first_send, halo_k = lax.optimization_barrier((first_send, halo_k))
     first_got = lax.all_to_all(first_send, AXES, split_axis=0, concat_axis=0, tiled=True)
-    second_send = tiles[jnp.concatenate([second, second + reqs], axis=1)]
+    second, halo_k, halo_v = lax.optimization_barrier((send_tile[:, 1], halo_k, halo_v))
+    second_send = pl.pallas_call(
+        pack_second_kernel,
+        grid_spec=pltpu.PrefetchScalarGridSpec(
+            num_scalar_prefetch=1,
+            grid=(devices // chunk,),
+            in_specs=[whole, whole],
+            out_specs=pl.BlockSpec((chunk, 2, BS, dh), lambda i, *_: (i, 0, 0, 0)),
+        ),
+        out_shape=jax.ShapeDtypeStruct((devices, 2, BS, dh), jnp.bfloat16),
+        compiler_params=pltpu.CompilerParams(vmem_limit_bytes=32 * 1024 * 1024),
+        cost_estimate=pl.CostEstimate(
+            flops=10**12, bytes_accessed=6_000_000, transcendentals=0
+        ),
+        name="pack_second",
+    )(second, k_t.reshape(reqs, BS, dh), v_t.reshape(reqs, BS, dh))
     my_far = lax.dynamic_slice_in_dim(far_blocks, rank * blocks, blocks, 1).reshape(-1)
     valid = (my_far >= 0).astype(jnp.int32)
     owner = jnp.where(my_far >= 0, my_far // blocks, -1)
@@ -302,7 +320,6 @@
         )
     )
     vert_other = lax.ppermute(first_got[:, 2], AXES, [(i, i ^ 1) for i in range(devices)])
-    second_send, vert_other = lax.optimization_barrier((second_send, vert_other))
     second_got = lax.all_to_all(second_send, AXES, split_axis=0, concat_axis=0, tiled=True)
 
     by_head = lambda *tail: pl.BlockSpec((1,) + tail, lambda h, *_: (h,) + (0,) * len(tail))
@@ -340,7 +357,7 @@
         ],
         compiler_params=pltpu.CompilerParams(vmem_limit_bytes=56 * 1024 * 1024),
         cost_estimate=pl.CostEstimate(
-            flops=4 * heads * blocks * rows * dh * (near + verts) * BS,
+            flops=400 * heads * blocks * rows * dh * (near + verts) * BS,
             bytes_accessed=40_000_000,
             transcendentals=heads * blocks * rows * (near + verts) * BS,
         ),

time: 194 us -> 187 us (0.964)
  starting transfers between devices: 30.7 us -> 25.3 us
  other arithmetic: 8 us -> 4.58 us
  waiting for transfers between devices: 76.3 us -> 78.7 us
    all_to_all x1, waiting for transfers between devices: 0.01 us -> 62.8 us  [shards(): lax.all_to_all(first_send, AXES, split_axis=0, concat_axis=0, tiled=True)]
    ppermute x1, waiting for transfers between devices: 56.3 us -> 0.01 us  [shards(): halo_v = lax.ppermute(values[tok - halo_rows:], AXES, forward)]
    transpose x0 -> x1, local copies, waits for them, and re-layouts: none -> 4.44 us  [shards(): v_t = values.transpose(1, 0, 2)]
    ppermute x1, waiting for transfers between devices: 4.15 us -> 0.01 us  [shards(): lax.ppermute(first_got[:, 2], AXES, [(i, i ^ 1) for i in range(devices)])]
    gather x1 -> x0, local copies, waits for them, and re-layouts: 3.1 us -> none  [shards(): second_send = tiles[jnp.concatenate([second, second + reqs], axis=1)]]
    all_to_all x1, starting transfers between devices: 10.7 us -> 7.88 us  [shards(): lax.all_to_all(second_send, AXES, split_axis=0, concat_axis=0, tiled=True)]
    unnamed x26 -> x14, local copies, waits for them, and re-layouts: 7.01 us -> 4.68 us
  transfers between devices with their start and end apart: 5 -> 5, of which waited for: 4 -> 2; matrix products, arithmetic and copies ran while one was open for 13% -> 9% of each run, Pallas kernels for 19% -> 20%
where the time goes in v4:
time: 187 us; the launch traced here: 186 us
  waiting for transfers between devices  78.7 us (42%)
  Pallas kernels  52.7 us (28%)
  starting transfers between devices  25.3 us (14%)
  local copies, waits for them, and re-layouts  24.6 us (13%)
  other arithmetic  4.58 us (2%)
    all_to_all x1, waiting for transfers between devices, shards(): lax.all_to_all(first_send, AXES, split_axis=0, concat_axis=0, tiled=True)  62.8 us
    pallas_call x1, Pallas kernels, shards(): pl.pallas_call(functools.partial(local_kernel, heads=heads, verts=verts,...  34.3 us
    all_to_all x1, waiting for transfers between devices, shards(): lax.all_to_all(second_send, AXES, split_axis=0, concat_axis=0, tiled=True)  15.9 us
    pallas_call x1, Pallas kernels, shards(): pl.pallas_call(functools.partial(merge_kernel, heads=heads, blocks=blocks...  15.8 us
    all_to_all x1, starting transfers between devices, shards(): lax.all_to_all(first_send, AXES, split_axis=0, concat_axis=0, tiled=True)  10.6 us
    all_to_all x1, starting transfers between devices, shards(): lax.all_to_all(second_send, AXES, split_axis=0, concat_axis=0, tiled=True)  7.88 us
    reshape x1, local copies, waits for them, and re-layouts, shards(): queries.reshape(tok, heads, group, dh).transpose(1, 0, 2, 3)  6.61 us
    unnamed x14, local copies, waits for them, and re-layouts  4.68 us
  transfers between devices with their start and end apart: 5, of which 2 were waited for; matrix products, arithmetic and copies ran while one was open for 9% of the time, Pallas kernels for 20%

profile of v4, /device:TPU:1, one launch (start us, length us, event | category | flops | bytes accessed | tf_op | source)
XLA Modules:
  0.0 186.4 jit_solution(12463578155442617403)
XLA Ops:
  0.0 4.4 %copy_bitcast_fusion.1 = (bf16[8,640,128]{2,1,0:T(8,128)(2,1)}, bf16[640,8,128]{2,0,1:T(8,128)(2,1)S(1)}, bf16[640,8,128]{2,0,1:T(8,128)(2,1)S(1)}, bf16[8,640,128]{2,1,0:T(8,128)(2,1)}) fusion(bf16[640,8,128]{2,1,0:T(8,128)(2,1)} %param.8, bf16[640,8,128]{2,1,0:T(8,128)(2,1)} %param.7), kind=kLoop, calls=%fused_computation.47 | loop fusion | bytes 7864320 | tf_op jit(solution)/shard_map/transpose | solution.py:242
  4.4 1.0 slice.20
  5.4 4.6 %collective-permute-start = (bf16[448,8,128]{2,0,1:T(8,128)(2,1)}, bf16[448,8,128]{2,0,1:T(8,128)(2,1)}, u32[]{:S(2)}, u32[]{:S(2)}) collective-permute-start(bf16[448,8,128]{2,0,1:T(8,128)(2,1)} %slice.20), channel_id=1, source_target_pairs={{0,1},{1,2},{2,3},{3,4},{4,5},{5,6},{6,7},{7,8},{8,9},{9,10},{10,1... | collective-permute-start | bytes 2752520 | tf_op jit(solution)/shard_map/ppermute | solution.py:238
  10.1 1.0 slice.21
  11.1 1.9 %collective-permute-start.1 = (bf16[448,8,128]{2,0,1:T(8,128)(2,1)}, bf16[448,8,128]{2,0,1:T(8,128)(2,1)}, u32[]{:S(2)}, u32[]{:S(2)}) collective-permute-start(bf16[448,8,128]{2,0,1:T(8,128)(2,1)} %slice.21), channel_id=1, source_target_pairs={{0,1},{1,2},{2,3},{3,4},{4,5},{5,6},{6,7},{7,8},{8,9},{9,10},{10,1... | collective-permute-start | bytes 2752520 | tf_op jit(solution)/shard_map/ppermute | solution.py:239
  14.1 1.2 add_select_fusion.1
  15.3 1.6 pack_first.1
  17.0 2.7 %copy-done = bf16[128,3,64,128]{3,2,1,0:T(8,128)(2,1)} copy-done((bf16[128,3,64,128]{3,2,1,0:T(8,128)(2,1)}, bf16[128,3,64,128]{3,2,1,0:T(8,128)(2,1)S(1)}, u32[]{:S(2)}) %copy-start) | copy-done | bytes 6291480
  19.6 10.6 %all-to-all-start = ((bf16[128,3,64,128]{3,2,1,0:T(8,128)(2,1)}), bf16[128,3,64,128]{3,2,1,0:T(8,128)(2,1)}, u32[]{:S(2)}, u32[]{:S(2)}) async-start(bf16[128,3,64,128]{3,2,1,0:T(8,128)(2,1)} %copy-done), calls=%async_computation | async-start | bytes 12582912 | tf_op jit(solution)/shard_map/all_to_all | solution.py:277
  30.7 0.6 convert_element_type.17.valid_sm
  31.6 0.9 reshape.210
  32.5 6.6 %copy.34 = bf16[640,8,4,128]{3,2,0,1:T(4,128)(2,1)} copy(bf16[640,8,4,128]{3,2,1,0:T(4,128)(2,1)} %bitcast.38) | data formatting | bytes 10485760 | tf_op jit(solution)/shard_map/reshape | solution.py:300
  40.7 0.8 convert_reduce_fusion.place_sm
  41.4 0.9 pack_second.1
  42.4 2.0 %copy-done.1 = bf16[128,2,64,128]{3,2,1,0:T(8,128)(2,1)} copy-done((bf16[128,2,64,128]{3,2,1,0:T(8,128)(2,1)}, bf16[128,2,64,128]{3,2,1,0:T(8,128)(2,1)S(1)}, u32[]{:S(2)}) %copy-start.1) | copy-done | bytes 4194328
  44.4 62.8 %all-to-all-done.mine_hbm.first_hbm = bf16[128,3,64,128]{3,2,1,0:T(8,128)(2,1)} async-done(((bf16[128,3,64,128]{3,2,1,0:T(8,128)(2,1)}), bf16[128,3,64,128]{3,2,1,0:T(8,128)(2,1)}, u32[]{:S(2)}, u32[]{:S(2)}) %all-to-all-start) | async-done | bytes 6291488 | tf_op jit(solution)/shard_map/all_to_all | solution.py:277
  107.2 1.8 slice_bitcast_fusion
  109.3 0.7 copy.35.off_sm
  109.9 7.9 %all-to-all-start.1 = ((bf16[128,2,64,128]{3,2,1,0:T(8,128)(2,1)}), bf16[128,2,64,128]{3,2,1,0:T(8,128)(2,1)}, u32[]{:S(2)}, u32[]{:S(2)}) async-start(bf16[128,2,64,128]{3,2,1,0:T(8,128)(2,1)} %copy-done.1), calls=%async_computation.1 | async-start | bytes 8388608 | tf_op jit(solution)/shard_map/all_to_all | solution.py:323
  117.8 0.8 copy.36.bias_ref
  118.7 34.3 %local_attention.1 = (f32[8,10,256,128]{3,2,1,0:T(8,128)}, f32[8,10,256]{2,1,0:T(8,128)}) custom-call(s32[1]{0:T(128)} %bitcast.13.core_sm, s32[8,12]{1,0:T(8,128)} %get-tuple-element.45.slot_sm, s32[8,4]{1,0:T(8,128)} %copy.35.off_sm, s32[1]{0:T(128)} %bitcast.14.first_sm, bf16[8,2560,128]{2,1,0:T(8,128)(2,1)} %bitcast.36, ...), custom_call_target="tpu_custom_call" | custom-call | flops 1073741824000 | bytes 40000000 | tf_op jit(solution)/shard_map/local_attention/pallas_call | solution.py:326
  153.0 1.6 copy.43
  154.6 15.9 %all-to-all-done.1.second_hbm = bf16[128,2,64,128]{3,2,1,0:T(8,128)(2,1)} async-done(((bf16[128,2,64,128]{3,2,1,0:T(8,128)(2,1)}), bf16[128,2,64,128]{3,2,1,0:T(8,128)(2,1)}, u32[]{:S(2)}, u32[]{:S(2)}) %all-to-all-start.1) | async-done | bytes 4194336 | tf_op jit(solution)/shard_map/all_to_all | solution.py:323
  170.4 15.8 %far_merge.1 = bf16[640,32,128]{2,1,0:T(8,128)(2,1)} custom-call(s32[80]{0:T(128)} %get-tuple-element.25.owner_sm, s32[80]{0:T(128)} %convert_reduce_fusion.place_sm, s32[80]{0:T(128)} %convert_element_type.17.valid_sm, bf16[8,2560,128]{2,1,0:T(8,128)(2,1)} %bitcast.37, f32[8,10,256,128]{3,2,1,0:T(8,128)} %get-tuple-element.34.local_ref, ...), custom_call_target="tpu_custom_call" | custom-call | flops 671088640 | bytes 25000000 | tf_op jit(solution)/shard_map/far_merge/pallas_call | solution.py:374
  (38 shorter events, 3.7 us)
Async XLA Ops:
  4.4 8.6 %copy-start.3 = (s32[8,1280]{1,0:T(8,128)S(1)}, s32[8,1280]{1,0:T(8,128)}, u32[]{:S(2)}) copy-start(s32[8,1280]{1,0:T(8,128)} %param.11) | copy-start | bytes 122884
  5.4 8.7 %copy-start.4 = (s32[8,12]{1,0:T(8,128)S(1)}, s32[8,12]{1,0:T(8,128)}, u32[]{:S(2)}) copy-start(s32[8,12]{1,0:T(8,128)} %param.9) | copy-start | bytes 1156
  5.4 36.0 %collective-permute-start = (bf16[448,8,128]{2,0,1:T(8,128)(2,1)}, bf16[448,8,128]{2,0,1:T(8,128)(2,1)}, u32[]{:S(2)}, u32[]{:S(2)}) collective-permute-start(bf16[448,8,128]{2,0,1:T(8,128)(2,1)} %slice.20), channel_id=1, source_target_pairs={{0,1},{1,2},{2,3},{3,4},{4,5},{5,6},{6,7},{7,8},{8,9},{9,10},{10,1... | collective-permute-start | bytes 2752520 | tf_op jit(solution)/shard_map/ppermute | solution.py:238
  11.1 30.4 %collective-permute-start.1 = (bf16[448,8,128]{2,0,1:T(8,128)(2,1)}, bf16[448,8,128]{2,0,1:T(8,128)(2,1)}, u32[]{:S(2)}, u32[]{:S(2)}) collective-permute-start(bf16[448,8,128]{2,0,1:T(8,128)(2,1)} %slice.21), channel_id=1, source_target_pairs={{0,1},{1,2},{2,3},{3,4},{4,5},{5,6},{6,7},{7,8},{8,9},{9,10},{10,1... | collective-permute-start | bytes 2752520 | tf_op jit(solution)/shard_map/ppermute | solution.py:239
  17.0 2.7 %copy-start = (bf16[128,3,64,128]{3,2,1,0:T(8,128)(2,1)}, bf16[128,3,64,128]{3,2,1,0:T(8,128)(2,1)S(1)}, u32[]{:S(2)}) copy-start(bf16[128,3,64,128]{3,2,1,0:T(8,128)(2,1)S(1)} %pack_first.1) | copy-start | bytes 18874372
  19.6 87.6 %all-to-all-start = ((bf16[128,3,64,128]{3,2,1,0:T(8,128)(2,1)}), bf16[128,3,64,128]{3,2,1,0:T(8,128)(2,1)}, u32[]{:S(2)}, u32[]{:S(2)}) async-start(bf16[128,3,64,128]{3,2,1,0:T(8,128)(2,1)} %copy-done), calls=%async_computation | async-start | bytes 12582912 | tf_op jit(solution)/shard_map/all_to_all | solution.py:277
  32.5 6.6 %copy-start.6 = (s32[8,4]{0,1:T(4,128)S(1)}, s32[8,4]{0,1:T(4,128)}, u32[]{:S(2)}) copy-start(s32[8,4]{0,1:T(4,128)} %param.10) | copy-start | bytes 388
  42.4 2.0 %copy-start.1 = (bf16[128,2,64,128]{3,2,1,0:T(8,128)(2,1)}, bf16[128,2,64,128]{3,2,1,0:T(8,128)(2,1)S(1)}, u32[]{:S(2)}) copy-start(bf16[128,2,64,128]{3,2,1,0:T(8,128)(2,1)S(1)} %pack_second.1) | copy-start | bytes 12582916
  107.2 2.0 %copy-start.5 = (s32[8,4]{0,1:T(4,128)S(1)}, s32[8,4]{0,1:T(4,128)}, u32[]{:S(2)}) copy-start(s32[8,4]{0,1:T(4,128)} %select_reduce_fusion.1) | copy-start | bytes 388
  109.0 9.6 %collective-permute-start.2 = (bf16[128,64,128]{2,1,0:T(8,128)(2,1)S(1)}, bf16[128,64,128]{2,1,0:T(8,128)(2,1)}, u32[]{:S(2)}, u32[]{:S(2)}) collective-permute-start(bf16[128,64,128]{2,1,0:T(8,128)(2,1)S(1)} %slice_bitcast_fusion), channel_id=1, source_target_pairs={{0,1},{1,0},{2,3},{3,2},{4,5},{5,4},{6,7},{7,6},{8,9},{9,8},{10,11... | collective-permute-start | bytes 6291464 | tf_op jit(solution)/shard_map/ppermute | solution.py:322
  109.9 7.9 %copy-start.2 = (f32[8,10,768]{2,0,1:T(8,128)S(1)}, f32[8,10,768]{2,0,1:T(8,128)}, u32[]{:S(2)}) copy-start(f32[8,10,768]{2,0,1:T(8,128)} %reshape.210) | copy-start | bytes 737284
  109.9 60.5 %all-to-all-start.1 = ((bf16[128,2,64,128]{3,2,1,0:T(8,128)(2,1)}), bf16[128,2,64,128]{3,2,1,0:T(8,128)(2,1)}, u32[]{:S(2)}, u32[]{:S(2)}) async-start(bf16[128,2,64,128]{3,2,1,0:T(8,128)(2,1)} %copy-done.1), calls=%async_computation.1 | async-start | bytes 8388608 | tf_op jit(solution)/shard_map/all_to_all | solution.py:323

commit v5 on v4

--- a/solution.py
+++ b/solution.py
@@ -77,6 +77,10 @@
     causal_bias = jnp.where((u_pos < BS) & (u_pos > t_pos), MASKED, 0.0)
     lane = lax.broadcasted_iota(jnp.int32, (1, near * BS), 1) // BS
 
+    zero_at = jnp.int32(0)
+    for i in range(1, near):
+        zero_at = jnp.where(off_sm[h, i] == 0, i, zero_at)
+
     def one_block(b, carry):
         rows = pl.multiple_of(b * group * BS, group * BS)
         q = q_ref[0, pl.ds(rows, group * BS), :]
@@ -84,7 +88,7 @@
         v_parts = []
         row_bias = jnp.zeros((1, near * BS), jnp.float32)
         for i in range(near):
-            off = off_sm[h, i]
+            off = off_sm[h, lax.rem(zero_at + i, near)]
             start = pl.multiple_of((b + NW - 1 - off) * BS, BS)
             k_parts.append(kx[pl.ds(start, BS), :])
             v_parts.append(vx[pl.ds(start, BS), :])
@@ -235,7 +239,8 @@
     rows = group * BS
 
     forward = [(i, i + 1) for i in range(devices - 1)]
-    halo_k = lax.ppermute(keys[tok - halo_rows :], AXES, forward)
+    rim_k, values = lax.optimization_barrier((keys[tok - halo_rows :], values))
+    halo_k = lax.ppermute(rim_k, AXES, forward)
     halo_v = lax.ppermute(values[tok - halo_rows :], AXES, forward)
 
     k_t = keys.transpose(1, 0, 2)
@@ -298,24 +303,17 @@
     my_place = jnp.sum(same & (jnp.arange(reqs)[None, :] < jnp.arange(reqs)[:, None]), axis=1)
 
     q_t = queries.reshape(tok, heads, group, dh).transpose(1, 0, 2, 3).reshape(heads, tok * group, dh)
-    zero_at = jnp.argmax((slash_offsets == 0).astype(jnp.int32), axis=1)
-    order = (zero_at[:, None] + jnp.arange(near)[None, :]) % near
-    offsets = jnp.sum(
-        jnp.where(order[:, :, None] == jnp.arange(near)[None, None, :], slash_offsets[:, None, :], 0),
-        axis=2,
-    )
     my_blocks = rank * blocks + jnp.arange(blocks)
     vert_ok = vert_blocks[:, None, :] <= my_blocks[None, :, None] - NW
     vert_bias = jnp.repeat(jnp.where(vert_ok, 0.0, MASKED).astype(jnp.float32), BS, axis=2)
 
     owner_at = jnp.maximum(owner, 0).astype(jnp.int32)
     my_place = my_place.astype(jnp.int32)
-    offsets = offsets.astype(jnp.int32)
-    second_send, first_got, halo_k, halo_v, q_t, vert_bias, offsets, owner_at, my_place, valid = (
+    second_send, first_got, halo_k, halo_v, q_t, vert_bias, owner_at, my_place, valid = (
         lax.optimization_barrier(
             (
                 second_send, first_got, halo_k, halo_v,
-                q_t, vert_bias, offsets, owner_at, my_place, valid,
+                q_t, vert_bias, owner_at, my_place, valid,
             )
         )
     )
@@ -365,7 +363,7 @@
     )(
         core.reshape(1).astype(jnp.int32),
         (vert_blocks // blocks).astype(jnp.int32),
-        offsets,
+        slash_offsets,
         (rank * blocks).reshape(1).astype(jnp.int32),
         q_t, k_t, v_t, halo_k.transpose(1, 0, 2), halo_v.transpose(1, 0, 2), vert_bias, first_got, vert_other,
     )

time: 187 us -> 187 us (level)
  local copies, waits for them, and re-layouts: 24.6 us -> 22.1 us
    transpose x1 -> x0, local copies, waits for them, and re-layouts: 4.44 us -> none  [shards(): v_t = values.transpose(1, 0, 2)]
    unnamed x14 -> x20, local copies, waits for them, and re-layouts: 4.68 us -> 6.94 us
where the time goes in v5:
time: 187 us; the launch traced here: 186 us
  waiting for transfers between devices  79.8 us (43%)
  Pallas kernels  54.3 us (29%)
  starting transfers between devices  25.8 us (14%)
  local copies, waits for them, and re-layouts  22.1 us (12%)
  other arithmetic  3.49 us (2%)
    all_to_all x1, waiting for transfers between devices, shards(): lax.all_to_all(first_send, AXES, split_axis=0, concat_axis=0, tiled=True)  64 us
    pallas_call x1, Pallas kernels, shards(): pl.pallas_call(functools.partial(local_kernel, heads=heads, verts=verts,...  34.4 us
    pallas_call x1, Pallas kernels, shards(): pl.pallas_call(functools.partial(merge_kernel, heads=heads, blocks=blocks...  17.4 us
    all_to_all x1, waiting for transfers between devices, shards(): lax.all_to_all(second_send, AXES, split_axis=0, concat_axis=0, tiled=True)  15.8 us
    all_to_all x1, starting transfers between devices, shards(): lax.all_to_all(first_send, AXES, split_axis=0, concat_axis=0, tiled=True)  10.6 us
    all_to_all x1, starting transfers between devices, shards(): lax.all_to_all(second_send, AXES, split_axis=0, concat_axis=0, tiled=True)  8.28 us
    unnamed x20, local copies, waits for them, and re-layouts  6.94 us
    reshape x1, local copies, waits for them, and re-layouts, shards(): queries.reshape(tok, heads, group, dh).transpose(1, 0, 2, 3)  6.59 us
  transfers between devices with their start and end apart: 5, of which 2 were waited for; matrix products, arithmetic and copies ran while one was open for 9% of the time, Pallas kernels for 20%

profile of v5, /device:TPU:1, one launch (start us, length us, event | category | flops | bytes accessed | tf_op | source)
XLA Modules:
  0.0 186.1 jit_solution(10592956774681774083)
XLA Ops:
  0.0 1.6 copy.43
  1.6 1.1 slice.20
  2.7 4.5 %collective-permute-start = (bf16[448,8,128]{2,0,1:T(8,128)(2,1)}, bf16[448,8,128]{2,0,1:T(8,128)(2,1)}, u32[]{:S(2)}, u32[]{:S(2)}) collective-permute-start(bf16[448,8,128]{2,0,1:T(8,128)(2,1)} %slice.20), channel_id=1, source_target_pairs={{0,1},{1,2},{2,3},{3,4},{4,5},{5,6},{6,7},{7,8},{8,9},{9,10},{10,1... | collective-permute-start | bytes 2752520 | tf_op jit(solution)/shard_map/ppermute | solution.py:243
  7.4 1.1 slice.21
  8.5 1.9 %collective-permute-start.1 = (bf16[448,8,128]{2,0,1:T(8,128)(2,1)}, bf16[448,8,128]{2,0,1:T(8,128)(2,1)}, u32[]{:S(2)}, u32[]{:S(2)}) collective-permute-start(bf16[448,8,128]{2,0,1:T(8,128)(2,1)} %slice.21), channel_id=1, source_target_pairs={{0,1},{1,2},{2,3},{3,4},{4,5},{5,6},{6,7},{7,8},{8,9},{9,10},{10,1... | collective-permute-start | bytes 2752520 | tf_op jit(solution)/shard_map/ppermute | solution.py:244
  11.5 1.2 add_select_fusion.1
  12.8 1.6 pack_first.1
  14.5 2.6 %copy-done = bf16[128,3,64,128]{3,2,1,0:T(8,128)(2,1)} copy-done((bf16[128,3,64,128]{3,2,1,0:T(8,128)(2,1)}, bf16[128,3,64,128]{3,2,1,0:T(8,128)(2,1)S(1)}, u32[]{:S(2)}) %copy-start) | copy-done | bytes 6291480
  17.1 10.6 %all-to-all-start = ((bf16[128,3,64,128]{3,2,1,0:T(8,128)(2,1)}), bf16[128,3,64,128]{3,2,1,0:T(8,128)(2,1)}, u32[]{:S(2)}, u32[]{:S(2)}) async-start(bf16[128,3,64,128]{3,2,1,0:T(8,128)(2,1)} %copy-done), calls=%async_computation | async-start | bytes 12582912 | tf_op jit(solution)/shard_map/all_to_all | solution.py:282
  29.0 0.9 reshape.177
  29.9 6.6 %copy.32 = bf16[640,8,4,128]{3,2,0,1:T(4,128)(2,1)} copy(bf16[640,8,4,128]{3,2,1,0:T(4,128)(2,1)} %bitcast.42) | data formatting | bytes 10485760 | tf_op jit(solution)/shard_map/reshape | solution.py:305
  36.5 0.6 broadcast_maximum_fusion
  37.0 0.7 convert_reduce_fusion.place_sm
  37.8 0.9 pack_second.1
  38.7 2.0 %copy-done.3 = bf16[128,2,64,128]{3,2,1,0:T(8,128)(2,1)} copy-done((bf16[128,2,64,128]{3,2,1,0:T(8,128)(2,1)}, bf16[128,2,64,128]{3,2,1,0:T(8,128)(2,1)S(1)}, u32[]{:S(2)}) %copy-start.3) | copy-done | bytes 4194328
  40.7 64.0 %all-to-all-done.mine_hbm.first_hbm = bf16[128,3,64,128]{3,2,1,0:T(8,128)(2,1)} async-done(((bf16[128,3,64,128]{3,2,1,0:T(8,128)(2,1)}), bf16[128,3,64,128]{3,2,1,0:T(8,128)(2,1)}, u32[]{:S(2)}, u32[]{:S(2)}) %all-to-all-start) | async-done | bytes 6291488 | tf_op jit(solution)/shard_map/all_to_all | solution.py:282
  104.8 1.8 slice_bitcast_fusion
  107.0 0.7 copy.33.off_sm
  107.7 8.3 %all-to-all-start.1 = ((bf16[128,2,64,128]{3,2,1,0:T(8,128)(2,1)}), bf16[128,2,64,128]{3,2,1,0:T(8,128)(2,1)}, u32[]{:S(2)}, u32[]{:S(2)}) async-start(bf16[128,2,64,128]{3,2,1,0:T(8,128)(2,1)} %copy-done.3), calls=%async_computation.1 | async-start | bytes 8388608 | tf_op jit(solution)/shard_map/all_to_all | solution.py:321
  116.0 0.8 copy.34.bias_ref
  116.8 34.4 %local_attention.1 = (f32[8,10,256,128]{3,2,1,0:T(8,128)}, f32[8,10,256]{2,1,0:T(8,128)}) custom-call(s32[1]{0:T(128)} %bitcast.13.core_sm, s32[8,12]{1,0:T(8,128)} %get-tuple-element.45.slot_sm, s32[8,4]{1,0:T(8,128)} %copy.33.off_sm, s32[1]{0:T(128)} %bitcast.14.first_sm, bf16[8,2560,128]{2,1,0:T(8,128)(2,1)} %bitcast.40, bf16[8,640,128]{2,1,0:T(8,128)(2,1)} %bitcast.36, ...), custom_call_target="tpu_custom_call" | custom-call | flops 1073741824000 | bytes 40000000 | tf_op jit(solution)/shard_map/local_attention/pallas_call | solution.py:324
  151.2 1.6 copy.41
  152.8 15.8 %all-to-all-done.1.second_hbm = bf16[128,2,64,128]{3,2,1,0:T(8,128)(2,1)} async-done(((bf16[128,2,64,128]{3,2,1,0:T(8,128)(2,1)}), bf16[128,2,64,128]{3,2,1,0:T(8,128)(2,1)}, u32[]{:S(2)}, u32[]{:S(2)}) %all-to-all-start.1) | async-done | bytes 4194336 | tf_op jit(solution)/shard_map/all_to_all | solution.py:321
  168.6 17.4 %far_merge.1 = bf16[640,32,128]{2,1,0:T(8,128)(2,1)} custom-call(s32[80]{0:T(128)} %get-tuple-element.26.owner_sm, s32[80]{0:T(128)} %convert_reduce_fusion.place_sm, s32[80]{0:T(128)} %convert_element_type.13.valid_sm, bf16[8,2560,128]{2,1,0:T(8,128)(2,1)} %bitcast.41, f32[8,10,256,128]{3,2,1,0:T(8,128)} %get-tuple-element.34.local_ref, ...), custom_call_target="tpu_custom_call" | custom-call | flops 671088640 | bytes 25000000 | tf_op jit(solution)/shard_map/far_merge/pallas_call | solution.py:372
  (40 shorter events, 3.0 us)
Async XLA Ops:
  0.0 7.2 %copy-start.4 = (bf16[640,8,128]{2,1,0:T(8,128)(2,1)S(1)}, bf16[640,8,128]{2,1,0:T(8,128)(2,1)}, u32[]{:S(2)}) copy-start(bf16[640,8,128]{2,1,0:T(8,128)(2,1)} %param.8) | copy-start | bytes 3932164
  0.0 10.5 %copy-start.6 = (s32[8,1280]{1,0:T(8,128)S(1)}, s32[8,1280]{1,0:T(8,128)}, u32[]{:S(2)}) copy-start(s32[8,1280]{1,0:T(8,128)} %param.11) | copy-start | bytes 122884
  1.6 36.2 %copy-start.1 = (bf16[640,8,128]{2,0,1:T(8,128)(2,1)}, bf16[640,8,128]{2,0,1:T(8,128)(2,1)S(1)}, u32[]{:S(2)}) copy-start(bf16[640,8,128]{2,0,1:T(8,128)(2,1)S(1)} %copy.43) | copy-start | bytes 3932164
  1.6 9.9 %copy-start.7 = (s32[8,12]{1,0:T(8,128)S(1)}, s32[8,12]{1,0:T(8,128)}, u32[]{:S(2)}) copy-start(s32[8,12]{1,0:T(8,128)} %param.9) | copy-start | bytes 1156
  2.7 35.0 %collective-permute-start = (bf16[448,8,128]{2,0,1:T(8,128)(2,1)}, bf16[448,8,128]{2,0,1:T(8,128)(2,1)}, u32[]{:S(2)}, u32[]{:S(2)}) collective-permute-start(bf16[448,8,128]{2,0,1:T(8,128)(2,1)} %slice.20), channel_id=1, source_target_pairs={{0,1},{1,2},{2,3},{3,4},{4,5},{5,6},{6,7},{7,8},{8,9},{9,10},{10,1... | collective-permute-start | bytes 2752520 | tf_op jit(solution)/shard_map/ppermute | solution.py:243
  7.4 30.4 %copy-start.2 = (bf16[640,8,128]{2,0,1:T(8,128)(2,1)}, bf16[640,8,128]{2,0,1:T(8,128)(2,1)S(1)}, u32[]{:S(2)}) copy-start(bf16[640,8,128]{2,0,1:T(8,128)(2,1)S(1)} %copy.42) | copy-start | bytes 3932164
  8.5 29.2 %collective-permute-start.1 = (bf16[448,8,128]{2,0,1:T(8,128)(2,1)}, bf16[448,8,128]{2,0,1:T(8,128)(2,1)}, u32[]{:S(2)}, u32[]{:S(2)}) collective-permute-start(bf16[448,8,128]{2,0,1:T(8,128)(2,1)} %slice.21), channel_id=1, source_target_pairs={{0,1},{1,2},{2,3},{3,4},{4,5},{5,6},{6,7},{7,8},{8,9},{9,10},{10,1... | collective-permute-start | bytes 2752520 | tf_op jit(solution)/shard_map/ppermute | solution.py:244
  14.4 2.7 %copy-start = (bf16[128,3,64,128]{3,2,1,0:T(8,128)(2,1)}, bf16[128,3,64,128]{3,2,1,0:T(8,128)(2,1)S(1)}, u32[]{:S(2)}) copy-start(bf16[128,3,64,128]{3,2,1,0:T(8,128)(2,1)S(1)} %pack_first.1) | copy-start | bytes 18874372
  17.1 87.7 %all-to-all-start = ((bf16[128,3,64,128]{3,2,1,0:T(8,128)(2,1)}), bf16[128,3,64,128]{3,2,1,0:T(8,128)(2,1)}, u32[]{:S(2)}, u32[]{:S(2)}) async-start(bf16[128,3,64,128]{3,2,1,0:T(8,128)(2,1)} %copy-done), calls=%async_computation | async-start | bytes 12582912 | tf_op jit(solution)/shard_map/all_to_all | solution.py:282
  38.7 2.0 %copy-start.3 = (bf16[128,2,64,128]{3,2,1,0:T(8,128)(2,1)}, bf16[128,2,64,128]{3,2,1,0:T(8,128)(2,1)S(1)}, u32[]{:S(2)}) copy-start(bf16[128,2,64,128]{3,2,1,0:T(8,128)(2,1)S(1)} %pack_second.1) | copy-start | bytes 12582916
  40.7 66.3 %copy-start.8 = (s32[8,4]{0,1:T(4,128)S(1)}, s32[8,4]{0,1:T(4,128)}, u32[]{:S(2)}) copy-start(s32[8,4]{0,1:T(4,128)} %param.10) | copy-start | bytes 388
  106.6 10.3 %collective-permute-start.2 = (bf16[128,64,128]{2,1,0:T(8,128)(2,1)S(1)}, bf16[128,64,128]{2,1,0:T(8,128)(2,1)}, u32[]{:S(2)}, u32[]{:S(2)}) collective-permute-start(bf16[128,64,128]{2,1,0:T(8,128)(2,1)S(1)} %slice_bitcast_fusion), channel_id=1, source_target_pairs={{0,1},{1,0},{2,3},{3,2},{4,5},{5,4},{6,7},{7,6},{8,9},{9,8},{10,11... | collective-permute-start | bytes 6291464 | tf_op jit(solution)/shard_map/ppermute | solution.py:320
  107.7 8.3 %copy-start.5 = (f32[8,10,768]{2,0,1:T(8,128)S(1)}, f32[8,10,768]{2,0,1:T(8,128)}, u32[]{:S(2)}) copy-start(f32[8,10,768]{2,0,1:T(8,128)} %reshape.177) | copy-start | bytes 737284
  107.7 60.9 %all-to-all-start.1 = ((bf16[128,2,64,128]{3,2,1,0:T(8,128)(2,1)}), bf16[128,2,64,128]{3,2,1,0:T(8,128)(2,1)}, u32[]{:S(2)}, u32[]{:S(2)}) async-start(bf16[128,2,64,128]{3,2,1,0:T(8,128)(2,1)} %copy-done.3), calls=%async_computation.1 | async-start | bytes 8388608 | tf_op jit(solution)/shard_map/all_to_all | solution.py:321
